TPU v7x, 32 devices: a whole 2x2x4 slice. The times are simulated.
32 devices in a mesh: section: 2 (over x), copy: 2 (over y), dp: 8 (over z, core).
Axes of the slice: x: 2, y: 2, z: 4, core: 2. Of those that a mesh axis runs over, the one named last changes fastest.
Arguments:
- boundary: bfloat16 [2, 2, 8, 1024, 512], P('section', None, 'dp', 'copy'), may hold values from -6 to 6
- sentence_ids: int32 [2, 8, 1024], P(None, 'dp'), may hold values from 0 to 31, never falling along the last dimension, each value on 1 to 64 neighbouring positions
- qkv_weight: bfloat16 [2, 512, 1536], P('section'), may hold values from -0.25 to 0.25
- out_weight: bfloat16 [2, 512, 512], P('section'), may hold values from -0.75 to 0.75
- inner_weight: bfloat16 [2, 512, 2048], P('section'), may hold values from -0.25 to 0.25
- outer_weight: bfloat16 [2, 2048, 512], P('section'), may hold values from -0.1875 to 0.1875
- norm_gain: float32 [2, 2, 512], P('section'), may hold values from 0.5 to 1.5
- norm_bias: float32 [2, 2, 512], P('section'), may hold values from -1.8 to 1.8
Outputs:
- result: bfloat16 [2, 2, 8, 1024, 512], P('section', None, 'dp', 'copy')
- grad_qkv: float32 [2, 512, 1536], P('section')
- grad_out: float32 [2, 512, 512], P('section')
- grad_inner: float32 [2, 512, 2048], P('section')
- grad_outer: float32 [2, 2048, 512], P('section')
- grad_gain: float32 [2, 2, 512], P('section')
- grad_bias: float32 [2, 2, 512], P('section')
Inputs may be any that keep to these rules, and one draw needn't show every extreme that they name: `sentence_ids`: along each row the ids never fall; each sentence spans 1 to 64 tokens, and in every draw some sentence spans exactly 64.
All inputs are finite; a program needn't handle non-finite values.
Results may differ from a plain program's by a relative error of at most 0.017.
Values may be sent and summed in bfloat16 or wider, within the bound.
A program may use at most 256 MiB of HBM per device.

v0:
```python
import functools

import jax
import jax.numpy as jnp
from jax import lax
from jax.experimental import pallas as pl
from jax.experimental.pallas import tpu as pltpu
from jax.sharding import PartitionSpec as P

HEADS = 8
REACH = 32
SPAN = 64
WINDOW = 256
NEG = -1e30
EPS = 1e-05
PIECES = 2
GROUPS = 3
BLOCKS = {1: ((0, 192, 0), (192, 80, 112), (272, 80, 192), (352, 192, 288)), 2: ((0, 160, 0), (160, 144, 48))}
MESH = pl.DeviceIdType.MESH
F32 = jnp.float32
BF16 = jnp.bfloat16


def mul(left, right):
    return jnp.dot(left, right, preferred_element_type=F32)


def against(left, right):
    return lax.dot_general(left, right, (((1,), (1,)), ((), ())), preferred_element_type=F32)


def contract(left, right):
    return lax.dot_general(left, right, (((0,), (0,)), ((), ())), preferred_element_type=F32)


def gelu(x):
    phi = 0.5 + 0.5 * lax.erf(x * 0.7071067811865476)
    bell = jnp.exp(x * x * -0.5) * 0.3989422804014327
    return (x * phi).astype(BF16), (phi + x * bell).astype(BF16)


def normalize(resid):
    center = resid - jnp.mean(resid, axis=-1, keepdims=True)
    spread = jnp.mean(center * center, axis=-1, keepdims=True)
    inverse = lax.rsqrt(spread + EPS)
    return center * inverse, inverse


def normalize_back(upstream, scaled, inverse, gain):
    tilted = upstream * gain
    first = jnp.mean(tilted, axis=-1, keepdims=True)
    second = jnp.mean(tilted * scaled, axis=-1, keepdims=True)
    return inverse * (tilted - first - scaled * second)


def halves(pair):
    lane = lax.broadcasted_iota(jnp.int32, pair.shape, 1)
    zero = jnp.zeros_like(pair)
    return jnp.where(lane < 64, pair, zero), jnp.where(lane < 64, zero, pair)


def kernel(
    units, rows, chips, width, inner_width,
    given, id_col, id_row, valid, w_qkv, w_out, w_in, w_outer, gains, shifts,
    result, summed, vectors,
    xb, ob, mixed, att, nlow, act, dg, one, two, inv_one, inv_two, goi, gai, gmix, probs,
    bias, gatt, hold, dkv, mine, sib, rsb, vec, slots,
    in_sem, out_sem, x_send, x_recv, sib_send, sib_recv, rs_send, rs_recv, ag_send, ag_recv,
    slot_send, slot_recv, pass_send, pass_recv, own_sem,
):
    blocks = BLOCKS[PIECES]
    section, copy, dp = lax.axis_index("section"), lax.axis_index("copy"), lax.axis_index("dp")
    core, layer = lax.rem(dp, 2), lax.div(dp, 2)
    line = chips // 2
    place = jnp.where(copy == 0, layer, chips - 1 - layer)

    def at(position):
        far = position >= line
        return (section, jnp.where(far, 1, 0), 2 * jnp.where(far, chips - 1 - position, position) + core)

    def around(position):
        return lax.rem(position + 2 * chips, chips)

    across = (1 - section, copy, dp)
    sibling = (section, copy, dp + 1 - 2 * core)
    ahead, behind = at(around(place + 1)), at(around(place - 1))

    vec[...] = jnp.zeros_like(vec)
    barrier = pltpu.get_barrier_semaphore()
    for other in (across, sibling, ahead, behind):
        pl.semaphore_signal(barrier, inc=1, device_id=other, device_id_type=MESH)
    load = pltpu.make_async_copy(given, xb.at[0], in_sem)
    load.start()
    load.wait()
    pl.semaphore_wait(barrier, 4)

    def unit_rows(unit):
        return pl.ds(pl.multiple_of(unit * rows, 16), rows)

    def x_copy(unit):
        span = unit_rows(unit)
        return pltpu.make_async_remote_copy(
            src_ref=ob.at[0, span], dst_ref=xb.at[1, span], send_sem=x_send.at[unit],
            recv_sem=x_recv.at[unit], device_id=across, device_id_type=MESH,
        )

    def forward(unit):
        span = unit_rows(unit)
        start = pl.multiple_of(unit * rows, 16)
        hidden = xb[section, span]
        scaled_qkv = mul(hidden, w_qkv[...])
        lane = lax.broadcasted_iota(jnp.int32, scaled_qkv.shape, 1)
        mixed[span] = jnp.where(lane < width, scaled_qkv * 0.125, scaled_qkv).astype(BF16)
        for index, (first, size, begin) in enumerate(blocks):
            allowed = id_col[unit, first : first + size] == id_row[unit, index : index + 1]
            bias[first : first + size] = jnp.where(allowed, 0.0, NEG)

        def pair_step(pair, _):
            lanes = pl.multiple_of(pair * 128, 128)
            for first, size, begin in blocks:
                near = pl.ds(pl.multiple_of(start + begin, 16), WINDOW)
                own = pl.ds(pl.multiple_of(start + first, 16), size)
                query = mixed[own, pl.ds(lanes, 128)]
                keys = halves(mixed[near, pl.ds(pl.multiple_of(width + pair * 128, 128), 128)])
                values = halves(mixed[near, pl.ds(pl.multiple_of(2 * width + pair * 128, 128), 128)])
                shares = []
                for head in range(2):
                    scores = against(query, keys[head]) + bias[first : first + size]
                    weights = jnp.exp(scores - jnp.max(scores, axis=-1, keepdims=True))
                    share = (weights * (1.0 / jnp.sum(weights, axis=-1, keepdims=True))).astype(BF16)
                    probs[own, pl.ds(pl.multiple_of(pair * 512 + head * 256, 256), 256)] = share
                    shares.append(share)
                attended = mul(jnp.concatenate(shares, axis=1), jnp.concatenate(values, axis=0))
                att[own, pl.ds(lanes, 128)] = attended.astype(BF16)
            return 0

        lax.fori_loop(0, width // 128, pair_step, 0)
        scaled, inverse = normalize(xb[section, span].astype(F32) + mul(att[span], w_out[...]))
        one[span] = scaled
        inv_one[span] = inverse
        normed = scaled * gains[0:1] + shifts[0:1]
        hold[...] = normed
        low = normed.astype(BF16)
        nlow[span] = low
        tile = 512
        count = inner_width // tile
        inner = mul(nlow[span], w_in[:, 0:tile])
        outer = hold[...]
        for step in range(count):
            ahead_inner = None
            if step + 1 < count:
                ahead_inner = mul(nlow[span], w_in[:, (step + 1) * tile : (step + 2) * tile])
            cols = pl.ds(step * tile, tile)
            active, slope = gelu(inner)
            act[span, cols] = active
            dg[span, cols] = slope
            outer = outer + mul(active, w_outer[cols])
            inner = ahead_inner
        scaled, inverse = normalize(outer)
        two[span] = scaled
        inv_two[span] = inverse
        ob[section, span] = (scaled * gains[1:2] + shifts[1:2]).astype(BF16)

    def backward(unit):
        span = unit_rows(unit)
        start = pl.multiple_of(unit * rows, 16)
        upstream = xb[1 - section, span].astype(F32) * valid[unit]
        scaled = two[span]
        vec[1:2] += jnp.sum(upstream * scaled, axis=0, keepdims=True)
        vec[3:4] += jnp.sum(upstream, axis=0, keepdims=True)
        grad_two = normalize_back(upstream, scaled, inv_two[span], gains[1:2])
        hold[...] = grad_two
        goi[span] = grad_two.astype(BF16)
        tile = 512
        count = inner_width // tile
        grad_active = against(goi[span], w_outer[0:tile])
        total = hold[...]
        for step in range(count):
            next_active = None
            if step + 1 < count:
                next_active = against(goi[span], w_outer[(step + 1) * tile : (step + 2) * tile])
            cols = pl.ds(step * tile, tile)
            grad_inner = (grad_active * dg[span, cols].astype(F32)).astype(BF16)
            dg[span, cols] = grad_inner
            total = total + against(grad_inner, w_in[:, step * tile : (step + 1) * tile])
            grad_active = next_active
        scaled = one[span]
        vec[0:1] += jnp.sum(total * scaled, axis=0, keepdims=True)
        vec[2:3] += jnp.sum(total, axis=0, keepdims=True)
        grad_one = normalize_back(total, scaled, inv_one[span], gains[0:1])
        hold[...] = grad_one
        low = grad_one.astype(BF16)
        gai[span] = low
        gatt[...] = against(low, w_out[...]).astype(BF16)

        def pair_step(pair, _):
            lanes = pl.multiple_of(pair * 128, 128)
            key_lanes = pl.ds(pl.multiple_of(width + pair * 128, 128), 128)
            value_lanes = pl.ds(pl.multiple_of(2 * width + pair * 128, 128), 128)
            dkv[...] = jnp.zeros_like(dkv)
            for first, size, begin in blocks:
                near = pl.ds(pl.multiple_of(start + begin, 16), WINDOW)
                own = pl.ds(pl.multiple_of(start + first, 16), size)
                queries = halves(mixed[own, pl.ds(lanes, 128)])
                keys = halves(mixed[near, key_lanes])
                values = halves(mixed[near, value_lanes])
                grad_pair = gatt[first : first + size, pl.ds(lanes, 128)]
                shares, grads = [], []
                for head in range(2):
                    share = probs[own, pl.ds(pl.multiple_of(pair * 512 + head * 256, 256), 256)]
                    wide = share.astype(F32)
                    grad_probs = against(grad_pair, values[head])
                    rowwise = jnp.sum(wide * grad_probs, axis=-1, keepdims=True)
                    grads.append((wide * (grad_probs - rowwise)).astype(BF16))
                    shares.append(share)
                grad_query = mul(jnp.concatenate(grads, axis=1), jnp.concatenate(keys, axis=0))
                gmix[own, pl.ds(lanes, 128)] = (grad_query * 0.125).astype(BF16)
                dkv[0, begin : begin + WINDOW] += contract(
                    jnp.concatenate(grads, axis=0), jnp.concatenate(queries, axis=0)
                )
                dkv[1, begin : begin + WINDOW] += contract(
                    jnp.concatenate(shares, axis=0), jnp.concatenate(halves(grad_pair), axis=0)
                )
            gmix[span, key_lanes] = dkv[0].astype(BF16)
            gmix[span, value_lanes] = dkv[1].astype(BF16)
            return 0

        lax.fori_loop(0, width // 128, pair_step, 0)
        ob[1 - section, span] = (hold[...] + against(gmix[span], w_qkv[...])).astype(BF16)

    def slot_step(slot, _):
        is_forward = jnp.where(section == 0, slot < units, lax.rem(slot, 2) == 0)
        unit = jnp.where(section == 0, lax.rem(slot, units), lax.div(slot, 2))

        @pl.when(is_forward)
        def _():
            @pl.when(section == 1)
            def _():
                x_copy(unit).wait_recv()

            forward(unit)

            @pl.when(section == 0)
            def _():
                x_copy(unit).start()

        @pl.when(jnp.logical_not(is_forward))
        def _():
            @pl.when(section == 0)
            def _():
                x_copy(unit).wait_recv()

            backward(unit)

            @pl.when(section == 1)
            def _():
                x_copy(unit).start()

        return 0

    lax.fori_loop(0, 2 * units, slot_step, 0)
    write = pltpu.make_async_copy(ob.at[1], result, out_sem)
    write.start()

    half = 1024
    seg = half // chips

    def sib_copy(group):
        return [
            pltpu.make_async_remote_copy(
                src_ref=probs.at[pl.ds(0, half), pl.ds(pl.multiple_of((group * 2 + way) * 256, 256), 256)],
                dst_ref=sib.at[group, way], send_sem=sib_send.at[group, way],
                recv_sem=sib_recv.at[group, way], device_id=sibling, device_id_type=MESH,
            )
            for way in range(2)
        ]

    def keep(group, block, value):
        value = value.astype(BF16)
        spot = pl.ds(pl.multiple_of(lax.rem(block, 2) * 512, 512), 512)
        here = lax.div(block, 2) == core

        @pl.when(here)
        def _():
            for way in range(2):
                mine[group, way, spot] = value[:, way * 256 : (way + 1) * 256]

        @pl.when(jnp.logical_not(here))
        def _():
            for way in range(2):
                cols = pl.ds((group * 2 + way) * 256, 256)
                probs[spot, cols] = value[:, way * 256 : (way + 1) * 256]

    def outer_block(block, _):
        cols = pl.ds(pl.multiple_of(block * 512, 512), 512)
        keep(0, block, contract(act[:, cols], goi[...]))
        return 0

    def inner_block(block, _):
        cols = pl.ds(pl.multiple_of(block * 512, 512), 512)
        keep(1, block, contract(nlow[...], dg[:, cols]))
        return 0

    def mixed_block(block, _):
        cols = pl.ds(pl.multiple_of((block - 1) * 512, 512), 512)
        keep(2, block, contract(xb[section], gmix[:, cols]))
        return 0

    def joined(group):
        for way, copy_of in enumerate(sib_copy(group)):
            copy_of.wait_recv()
            mine[group, way] = (mine[group, way].astype(F32) + sib[group, way].astype(F32)).astype(BF16)

    def segment(position):
        return pl.ds(pl.multiple_of(around(position) * seg, 16), seg)

    def target(way):
        return tuple(jnp.where(way == 0, a, b) for a, b in zip(ahead, behind))

    def rs_copy(group, way, step, source):
        return pltpu.make_async_remote_copy(
            src_ref=source, dst_ref=rsb.at[group, way, step], send_sem=rs_send.at[group, way, step],
            recv_sem=rs_recv.at[group, way, step], device_id=target(way), device_id_type=MESH,
        )

    def final_rows(position):
        return pl.ds(pl.multiple_of(core * half + around(position) * seg, 16), seg)

    def ag_copy(group, way, step, source, position):
        return pltpu.make_async_remote_copy(
            src_ref=source, dst_ref=summed.at[group, way, final_rows(position)],
            send_sem=ag_send.at[group, way, step], recv_sem=ag_recv.at[group, way, step],
            device_id=target(way), device_id_type=MESH,
        )

    def pass_copy(group, way, source, position):
        return pltpu.make_async_remote_copy(
            src_ref=source, dst_ref=summed.at[group, way, final_rows(position)],
            send_sem=pass_send.at[group, way], recv_sem=pass_recv.at[group, way],
            device_id=sibling, device_id_type=MESH,
        )

    def own_copy(group, way):
        sign = 1 - 2 * way
        return pltpu.make_async_copy(
            rsb.at[group, way, chips - 2], summed.at[group, way, final_rows(place + sign)],
            own_sem.at[group, way],
        )

    def ring(group, way, step):
        sign = 1 - 2 * way

        @pl.when(step == 0)
        def _():
            rs_copy(group, way, 0, mine.at[group, way, segment(place)]).start()

        @pl.when(jnp.logical_and(step >= 1, step < chips))
        def _():
            last = step - 1
            slot = rsb.at[group, way, last]
            rs_copy(group, way, last, slot).wait_recv()
            part = mine[group, way, segment(place - sign * step)]
            rsb[group, way, last] = (rsb[group, way, last].astype(F32) + part.astype(F32)).astype(BF16)

            @pl.when(step < chips - 1)
            def _():
                rs_copy(group, way, step, slot).start()

            @pl.when(step == chips - 1)
            def _():
                ag_copy(group, way, 0, slot, place + sign).start()
                pass_copy(group, way, slot, place + sign).start()
                own_copy(group, way).start()

        @pl.when(jnp.logical_and(step >= chips, step < 2 * chips - 1))
        def _():
            last = step - chips
            position = place - sign * last
            arrived = summed.at[group, way, final_rows(position)]
            ag_copy(group, way, last, arrived, position).wait_recv()

            @pl.when(last + 1 < chips - 1)
            def _():
                ag_copy(group, way, last + 1, arrived, position).start()

            pass_copy(group, way, arrived, position).start()

    def slot_copy(step):
        return pltpu.make_async_remote_copy(
            src_ref=slots.at[step], dst_ref=slots.at[step + 1], send_sem=slot_send.at[step],
            recv_sem=slot_recv.at[step], device_id=ahead, device_id_type=MESH,
        )

    vec_copy = pltpu.make_async_remote_copy(
        src_ref=vec.at[pl.ds(0, 8)], dst_ref=vec.at[pl.ds(8, 8)], send_sem=slot_send.at[chips],
        recv_sem=slot_recv.at[chips], device_id=sibling, device_id_type=MESH,
    )
    vec_copy.start()
    lax.fori_loop(0, 4, outer_block, 0)
    for copy_of in sib_copy(0):
        copy_of.start()
    lax.fori_loop(0, 4, inner_block, 0)
    for copy_of in sib_copy(1):
        copy_of.start()
    joined(0)
    for way in range(2):
        ring(0, way, 0)
    keep(2, 0, contract(att[...], gai[...]))
    lax.fori_loop(1, 4, mixed_block, 0)
    for copy_of in sib_copy(2):
        copy_of.start()
    joined(1)
    joined(2)
    vec_copy.wait()
    slots[0] = vec[0:8] + vec[8:16]

    def round_step(index, _):
        def each(flat, _):
            group, way = lax.div(flat, 2), lax.rem(flat, 2)
            step = jnp.where(group == 0, index, index - 1)

            @pl.when(step >= 0)
            def _():
                ring(group, way, step)

            return 0

        lax.fori_loop(0, 2 * GROUPS, each, 0)

        @pl.when(index < chips)
        def _():
            @pl.when(index > 1)
            def _():
                slot_copy(index - 2).wait_recv()

            slot_copy(index - 1).start()

        return 0

    lax.fori_loop(1, 2 * chips, round_step, 0)
    slot_copy(chips - 2).wait_recv()
    total = jnp.zeros((8, width), F32)
    for position in range(chips):
        total = total + slots[around(place - position)]
    vectors[...] = total

    def drain(flat, _):
        group, way = lax.div(flat, 2), lax.rem(flat, 2)
        own_copy(group, way).wait()

        def each(step, _):
            rs_copy(group, way, step, rsb.at[group, way, 0]).wait_send()
            ag_copy(group, way, step, rsb.at[group, way, 0], place).wait_send()
            return 0

        lax.fori_loop(0, chips - 1, each, 0)
        whole = pltpu.make_async_remote_copy(
            src_ref=summed.at[group, way, pl.ds(0, half)], dst_ref=summed.at[group, way, pl.ds(0, half)],
            send_sem=pass_send.at[group, way], recv_sem=pass_recv.at[group, way],
            device_id=sibling, device_id_type=MESH,
        )
        whole.wait_send()
        whole.wait_recv()
        return 0

    lax.fori_loop(0, 2 * GROUPS, drain, 0)
    for group in range(GROUPS):
        for copy_of in sib_copy(group):
            copy_of.wait_send()

    def drain_slots(step, _):
        slot_copy(step).wait_send()
        return 0

    lax.fori_loop(0, chips - 1, drain_slots, 0)

    def drain_units(unit, _):
        x_copy(unit).wait_send()
        return 0

    lax.fori_loop(0, units, drain_units, 0)
    write.wait()


def per_device(mesh, boundary, sentence_ids, qkv_weight, out_weight, inner_weight, outer_weight, norm_gain, norm_bias):
    micro, local, width = boundary.shape[1], boundary.shape[3], boundary.shape[4]
    inner_width = inner_weight.shape[2]
    length = sentence_ids.shape[2]
    chips = mesh.shape["copy"] * mesh.shape["dp"] // 2
    copy = lax.axis_index("copy")
    reach = local + REACH
    pieces = PIECES
    rows = reach if pieces == 1 else reach // 2 + REACH
    begins = (0,) if pieces == 1 else (0, reach - rows)
    units = micro * pieces
    tokens = units * rows
    own = boundary[0, :, 0]
    ids = sentence_ids[:, 0]

    def swap(strip):
        return lax.ppermute(strip, "copy", [(0, 1), (1, 0)])

    def split(whole):
        return jnp.stack([whole[m, b : b + rows] for m in range(micro) for b in begins])

    strip = lax.dynamic_slice_in_dim(own, (1 - copy) * (local - REACH), REACH, 1)
    strip = swap(strip)
    reaching = jnp.where(
        copy == 0, jnp.concatenate([own, strip], axis=1), jnp.concatenate([strip, own], axis=1)
    )
    given = split(reaching).reshape(tokens, width)
    start = copy * (local - REACH)
    near_ids = lax.dynamic_slice_in_dim(ids, start, reach, 1)
    unit_ids = split(near_ids)
    cuts = (local,) if pieces == 1 else (reach // 2, local, length - reach // 2)
    spot = jnp.arange(length)
    owner = sum((spot >= cut).astype(jnp.int32) for cut in cuts)[None]
    for index, cut in enumerate(cuts):
        crossing = ids == ids[:, cut - 1 : cut]
        left = jnp.sum(crossing & (spot < cut), axis=1, keepdims=True)
        right = jnp.sum(crossing & (spot >= cut), axis=1, keepdims=True)
        owner = jnp.where(crossing, jnp.where(left >= right, index, index + 1), owner)
    near_owner = lax.dynamic_slice_in_dim(owner, start, reach, 1) - copy * pieces
    valid = jnp.stack(
        [near_owner[m, b : b + rows] == j for m in range(micro) for j, b in enumerate(begins)]
    )
    id_row = jnp.stack([unit_ids[:, b : b + WINDOW] for _, _, b in BLOCKS[pieces]], axis=1)

    any_space = pl.BlockSpec(memory_space=pl.ANY)
    vmem = pl.BlockSpec(memory_space=pltpu.VMEM)
    dma = pltpu.SemaphoreType.DMA
    hops = chips - 1
    result, summed, vectors = pl.pallas_call(
        functools.partial(kernel, units, rows, chips, width, inner_width),
        out_shape=(
            jax.ShapeDtypeStruct((tokens, width), BF16),
            jax.ShapeDtypeStruct((GROUPS, 2, 2048, 256), BF16),
            jax.ShapeDtypeStruct((8, width), F32),
        ),
        in_specs=[any_space] + [vmem] * 9,
        out_specs=(any_space, any_space, vmem),
        scratch_shapes=[
            pltpu.VMEM((2, tokens, width), BF16),
            pltpu.VMEM((2, tokens, width), BF16),
            pltpu.VMEM((tokens, 3 * width), BF16),
            pltpu.VMEM((tokens, width), BF16),
            pltpu.VMEM((tokens, width), BF16),
            pltpu.VMEM((tokens, inner_width), BF16),
            pltpu.VMEM((tokens, inner_width), BF16),
            pltpu.VMEM((tokens, width), F32),
            pltpu.VMEM((tokens, width), F32),
            pltpu.VMEM((tokens, 1), F32),
            pltpu.VMEM((tokens, 1), F32),
            pltpu.VMEM((tokens, width), BF16),
            pltpu.VMEM((tokens, width), BF16),
            pltpu.VMEM((tokens, 3 * width), BF16),
            pltpu.VMEM((tokens, HEADS * WINDOW), BF16),
            pltpu.VMEM((rows, WINDOW), F32),
            pltpu.VMEM((rows, width), BF16),
            pltpu.VMEM((rows, width), F32),
            pltpu.VMEM((2, rows, 128), F32),
            pltpu.VMEM((GROUPS, 2, 1024, 256), BF16),
            pltpu.VMEM((GROUPS, 2, 1024, 256), BF16),
            pltpu.VMEM((GROUPS, 2, hops, 1024 // chips, 256), BF16),
            pltpu.VMEM((16, width), F32),
            pltpu.VMEM((chips, 8, width), F32),
            dma, dma, dma((units,)), dma((units,)), dma((GROUPS, 2)), dma((GROUPS, 2)),
            dma((GROUPS, 2, hops)), dma((GROUPS, 2, hops)), dma((GROUPS, 2, hops)), dma((GROUPS, 2, hops)),
            dma((chips + 1,)), dma((chips + 1,)), dma((GROUPS, 2)), dma((GROUPS, 2)), dma((GROUPS, 2)),
        ],
        compiler_params=pltpu.CompilerParams(
            collective_id=0, has_side_effects=True, vmem_limit_bytes=63 * 1024 * 1024
        ),
    )(
        given, unit_ids[:, :, None], id_row, valid[:, :, None].astype(F32),
        qkv_weight[0], out_weight[0], inner_weight[0], outer_weight[0], norm_gain[0], norm_bias[0],
    )

    parts = result.reshape(micro, pieces, rows, width)
    valid = valid.reshape(micro, pieces, rows, 1)
    merged, merged_valid = parts[:, 0], valid[:, 0]
    if pieces == 2:
        cut = begins[1]
        over = rows - cut
        blend = jnp.where(valid[:, 0, cut:], parts[:, 0, cut:], parts[:, 1, :over])
        merged = jnp.concatenate([parts[:, 0, :cut], blend, parts[:, 1, over:]], axis=1)
        merged_valid = jnp.concatenate(
            [valid[:, 0, :cut], valid[:, 0, cut:] | valid[:, 1, :over], valid[:, 1, over:]], axis=1
        )
    strip = swap(lax.dynamic_slice_in_dim(merged, (1 - copy) * local, REACH, 1))
    final = lax.dynamic_slice_in_dim(merged, copy * REACH, local, 1)
    final_valid = lax.dynamic_slice_in_dim(merged_valid, copy * REACH, local, 1)
    edge = (1 - copy) * (local - REACH)
    kept = jnp.where(
        lax.dynamic_slice_in_dim(final_valid, edge, REACH, 1),
        lax.dynamic_slice_in_dim(final, edge, REACH, 1), strip,
    )
    final = lax.dynamic_update_slice_in_dim(final, kept, edge, 1)

    wide = summed.astype(F32)
    joined = jnp.concatenate([wide[:, 0], wide[:, 1]], axis=-1)
    grad_inner = joined[1].reshape(4, 512, 512).transpose(1, 0, 2).reshape(width, inner_width)
    grad_qkv = joined[2, 512:].reshape(3, 512, 512).transpose(1, 0, 2).reshape(width, 3 * width)
    return (
        final[None, :, None], grad_qkv[None], joined[2, :512][None], grad_inner[None], joined[0][None],
        vectors[None, 0:2], vectors[None, 2:4],
    )


def solution(mesh):
    weight = P("section", None, None)
    edge = P("section", None, "dp", "copy", None)
    return jax.shard_map(
        functools.partial(per_device, mesh),
        mesh=mesh,
        in_specs=(edge, P(None, "dp", None)) + (weight,) * 6,
        out_specs=(edge,) + (weight,) * 6,
        check_vma=False,
    )
```

profile of v0, /device:TPU:0, one launch (start us, length us, event | category | flops | bytes accessed | tf_op | source)
XLA Modules:
  0.0 228.8 jit_solution(3398196079186251235)
XLA Ops:
  0.6 0.0 copy-start.3
  0.6 0.9 dynamic-slice_bitcast_fusion.1
  1.6 3.0 %collective-permute-start = (bf16[2,32,512]{2,1,0:T(8,128)(2,1)S(1)}, bf16[2,32,512]{2,1,0:T(8,128)(2,1)S(1)}, u32[]{:S(2)}, u32[]{:S(2)}) collective-permute-start(bf16[2,32,512]{2,1,0:T(8,128)(2,1)S(1)} %dynamic-slice_bitcast_fusion.1), channel_id=1, source_target_pairs={{0,8},{8,0},{1,9},{9,1},{2,10},{10,2},{3,11},{11,3},{4,12},{12,4},... | collective-permute-start | bytes 196616 | tf_op jit(solution)/shard_map/ppermute | solution.py:501
  4.6 0.7 copy.112
  5.3 0.8 constant_dynamic-slice_fusion.1
  6.1 0.1 dynamic-slice.2
  6.2 0.2 slice_reduce_fusion.2
  6.4 1.0 fusion.5
  7.4 0.1 fusion.10
  7.5 0.1 slice_compare_fusion.3
  7.6 0.1 fusion.23
  7.7 0.1 fusion.22
  7.8 0.1 fusion.21
  7.9 0.1 slice_bitcast_fusion.6
  8.0 0.2 copy.69
  8.2 0.2 copy.68
  8.4 0.2 copy.67
  8.6 0.2 copy.66
  8.7 1.1 copy.70.id_col
  9.8 0.6 pad_add_fusion.id_row
  10.5 0.9 add_convert_fusion.valid
  11.3 0.1 fusion.14
  11.4 0.0 collective-permute-done
  11.4 0.0 copy-done.3
  11.4 0.2 maximum_select_fusion
  11.7 0.1 fusion.20
  11.8 1.2 pad_maximum_fusion.1
  13.0 171.2 %shard_map.135 = (bf16[1216,512]{1,0:T(8,128)(2,1)}, bf16[3,2,2048,256]{3,2,1,0:T(8,128)(2,1)}, f32[8,512]{1,0:T(8,128)}) custom-call(bf16[1216,512]{1,0:T(8,128)(2,1)} %bitcast.94, s32[4,304,1]{2,1,0:T(8,128)} %copy.70.id_col, s32[4,2,256]{2,1,0:T(2,128)} %pad_add_fusion.id_row, f32[4,304,1]{2,1,0:T(8,128)} %add_convert_fusion.valid, ...), custom_call_target="tpu_custom_call" | custom-call | tf_op jit(solution)/shard_map/pallas_call | solution.py:533
  184.2 8.5 %convert_element_type.55 = f32[3,2,2048,256]{3,2,1,0:T(8,128)} convert(bf16[3,2,2048,256]{3,2,1,0:T(8,128)(2,1)} %get-tuple-element.11) | non-fusion elementwise | flops 3145728 | bytes 18874368 | tf_op jit(solution)/shard_map/convert_element_type | solution.py:600
  192.7 8.6 %slice_bitcast_fusion = (f32[3,2048,256]{2,1,0:T(8,128)S(1)}, f32[3,2048,256]{2,1,0:T(8,128)}) fusion(f32[3,2,2048,256]{3,2,1,0:T(8,128)} %convert_element_type.55), kind=kLoop, calls=%fused_computation.6 | loop fusion | bytes 25165824 | tf_op jit(solution)/shard_map/squeeze | solution.py:601
  201.3 3.7 %fusion.1 = f32[1,1536,512]{2,1,0:T(8,128)} fusion(f32[3,2048,256]{2,1,0:T(8,128)} %get-tuple-element.49, f32[3,2048,256]{2,1,0:T(8,128)S(1)} %get-tuple-element.48), kind=kLoop, calls=%fused_computation.10 | loop fusion | flops 786432 | bytes 15728640 | tf_op jit(solution)/shard_map/concatenate | solution.py:601
  205.0 0.1 copy-done
  205.1 2.4 %pad_maximum_fusion = (f32[1,2048,512]{2,1,0:T(8,128)}, f32[1,2048,512]{2,1,0:T(8,128)S(1)}) fusion(f32[3,2048,256]{2,1,0:T(8,128)S(1)} %get-tuple-element.48, f32[3,2048,256]{2,1,0:T(8,128)S(1)} %copy-done), kind=kLoop, calls=%fused_computation.9 | loop fusion | flops 2097152 | bytes 20971520 | tf_op jit(solution)/shard_map/concatenate | solution.py:601
  207.4 0.0 copy-done.4
  207.4 0.6 slice_bitcast_fusion.7
  208.1 0.0 copy-done.2
  208.1 0.1 slice_bitcast_fusion.3
  208.1 0.1 fusion.3
  208.2 0.1 pad_maximum_fusion.2
  208.3 1.2 dynamic-slice_bitcast_fusion
  209.5 1.2 collective-permute-start.1
  210.6 1.1 fusion.2
  211.8 4.6 %copy.81 = f32[512,4,512]{2,1,0:T(4,128)} copy(f32[512,4,512]{2,0,1:T(8,128)S(1)} %bitcast.91) | data formatting | bytes 8388608 | tf_op jit(solution)/shard_map/transpose | solution.py:602
  216.4 6.0 %broadcast_in_dim_reshape.7 = f32[1,512,2048]{2,1,0:T(8,128)} reshape(f32[512,4,512]{2,1,0:T(4,128)} %copy.81) | data formatting | bytes 8388608 | tf_op jit(solution)/shard_map/broadcast_in_dim;reshape | solution.py:605
  222.4 2.4 %copy.80 = f32[3,512,512]{1,2,0:T(8,128)S(1)} copy(f32[3,512,512]{2,1,0:T(8,128)} %bitcast.93) | data formatting | bytes 6291456 | tf_op jit(solution)/shard_map/reshape;squeeze | solution.py:603
  224.8 2.4 %copy.82 = f32[1,512,1536]{2,1,0:T(8,128)} copy(f32[1,512,1536]{1,2,0:T(8,128)S(1)} %bitcast.92) | data formatting | bytes 6291456
  227.2 0.0 collective-permute-done.1
  227.2 1.6 bitcast_dynamic-update-slice_fusion
  (24 shorter events, 0.1 us)
Async XLA Ops:
  0.6 10.8 %copy-start.3 = (bf16[1,2,1,512,512]{4,3,2,1,0:T(8,128)(2,1)S(1)}, bf16[1,2,1,512,512]{4,3,2,1,0:T(8,128)(2,1)}, u32[]{:S(2)}) copy-start(bf16[1,2,1,512,512]{4,3,2,1,0:T(8,128)(2,1)} %param.8) | copy-start | bytes 3145732
  1.6 9.9 %collective-permute-start = (bf16[2,32,512]{2,1,0:T(8,128)(2,1)S(1)}, bf16[2,32,512]{2,1,0:T(8,128)(2,1)S(1)}, u32[]{:S(2)}, u32[]{:S(2)}) collective-permute-start(bf16[2,32,512]{2,1,0:T(8,128)(2,1)S(1)} %dynamic-slice_bitcast_fusion.1), channel_id=1, source_target_pairs={{0,8},{8,0},{1,9},{9,1},{2,10},{10,2},{3,11},{11,3},{4,12},{12,4},... | collective-permute-start | bytes 196616 | tf_op jit(solution)/shard_map/ppermute | solution.py:501
  201.3 3.8 %copy-start = (f32[3,2048,256]{2,1,0:T(8,128)S(1)}, f32[3,2048,256]{2,1,0:T(8,128)}, u32[]{:S(2)}) copy-start(f32[3,2048,256]{2,1,0:T(8,128)} %get-tuple-element.49) | copy-start | bytes 18874372
  205.1 2.4 %copy-start.4 = (f32[8,512]{1,0:T(8,128)S(1)}, f32[8,512]{1,0:T(8,128)}, u32[]{:S(2)}) copy-start(f32[8,512]{1,0:T(8,128)} %get-tuple-element.12) | copy-start | bytes 49156
  205.1 3.0 %copy-start.2 = (bf16[1216,512]{1,0:T(8,128)(2,1)S(1)}, bf16[1216,512]{1,0:T(8,128)(2,1)}, u32[]{:S(2)}) copy-start(bf16[1216,512]{1,0:T(8,128)(2,1)} %get-tuple-element.10) | copy-start | bytes 3735556
  208.3 3.5 %copy-start.1 = (bf16[2,544,512]{2,1,0:T(8,128)(2,1)}, bf16[2,544,512]{2,1,0:T(8,128)(2,1)S(1)}, u32[]{:S(2)}) copy-start(bf16[2,544,512]{2,1,0:T(8,128)(2,1)S(1)} %pad_maximum_fusion.2) | copy-start | bytes 3342340
  209.5 17.7 %collective-permute-start.1 = (bf16[2,32,512]{2,1,0:T(8,128)(2,1)S(1)}, bf16[2,32,512]{2,1,0:T(8,128)(2,1)S(1)}, u32[]{:S(2)}, u32[]{:S(2)}) collective-permute-start(bf16[2,32,512]{2,1,0:T(8,128)(2,1)S(1)} %constant_dynamic-slice_fusion), channel_id=1, source_target_pairs={{0,8},{8,0},{1,9},{9,1},{2,10},{10,2},{3,11},{11,3},{4,12},{12,4},... | collective-permute-start | bytes 196616 | tf_op jit(solution)/shard_map/ppermute | solution.py:501
where the time goes:
time: 229 us
  Pallas kernels  171 us (75%)
  local copies, waits for them, and re-layouts  30.9 us (13%)
  other arithmetic  21.7 us (9%)
  starting transfers between devices  4.14 us (2%)
    pallas_call x1, Pallas kernels, per_device(): pl.pallas_call(functools.partial(kernel, units, rows, chips, width, inner...  171 us
    squeeze x1, local copies, waits for them, and re-layouts, per_device(): joined = jnp.concatenate([wide[:, 0], wide[:, 1]], axis=-1)  8.56 us
    convert_element_type x1, other arithmetic, per_device(): wide = summed.astype(F32)  8.5 us
    concatenate x3, other arithmetic, per_device(): joined = jnp.concatenate([wide[:, 0], wide[:, 1]], axis=-1)  7.21 us
    another operation x1, local copies, waits for them, and re-layouts, per_device(): grad_inner[None]  6.05 us
    transpose x1, local copies, waits for them, and re-layouts, per_device(): joined[1].reshape(4, 512, 512).transpose(1, 0, 2)  4.62 us
  transfers between devices with their start and end apart: 2, of which 0 were waited for; matrix products, arithmetic and copies ran while one was open for 10% of the time, Pallas kernels for 0%

commit v1 on v0

--- a/solution.py
+++ b/solution.py
@@ -9,13 +9,11 @@
 
 HEADS = 8
 REACH = 32
-SPAN = 64
 WINDOW = 256
 NEG = -1e30
 EPS = 1e-05
-PIECES = 2
 GROUPS = 3
-BLOCKS = {1: ((0, 192, 0), (192, 80, 112), (272, 80, 192), (352, 192, 288)), 2: ((0, 160, 0), (160, 144, 48))}
+BLOCKS = ((0, 160, 0), (160, 144, 48))
 MESH = pl.DeviceIdType.MESH
 F32 = jnp.float32
 BF16 = jnp.bfloat16
@@ -61,18 +59,27 @@
 
 def kernel(
     units, rows, chips, width, inner_width,
-    given, id_col, id_row, valid, w_qkv, w_out, w_in, w_outer, gains, shifts,
+    boundary, ids, qkv_weight, out_weight, inner_weight, outer_weight, gain_rows, shift_rows,
     result, summed, vectors,
-    xb, ob, mixed, att, nlow, act, dg, one, two, inv_one, inv_two, goi, gai, gmix, probs,
-    bias, gatt, hold, dkv, mine, sib, rsb, vec, slots,
-    in_sem, out_sem, x_send, x_recv, sib_send, sib_recv, rs_send, rs_recv, ag_send, ag_recv,
-    slot_send, slot_recv, pass_send, pass_recv, own_sem,
+    w_qkv, w_out, w_in, w_outer, info, column,
+    xb, ob, mixed, att, nlow, act, dg, one, two, inv_one, inv_two, goi, gai, gmix, probs, scale,
+    bias, gatt, hold, dkv, strip, mine, sib, rsb, vec, slots,
+    weight_sem, in_sem, out_sem, x_send, x_recv, y_send, y_recv, sib_send, sib_recv, rs_send, rs_recv,
+    ag_send, ag_recv, slot_send, slot_recv, pass_send, pass_recv, own_sem,
 ):
-    blocks = BLOCKS[PIECES]
+    blocks = BLOCKS
+    micro, local = boundary.shape[1], boundary.shape[3]
+    length = ids.shape[2]
+    reach = local + REACH
+    shift = reach - rows
     section, copy, dp = lax.axis_index("section"), lax.axis_index("copy"), lax.axis_index("dp")
     core, layer = lax.rem(dp, 2), lax.div(dp, 2)
     line = chips // 2
     place = jnp.where(copy == 0, layer, chips - 1 - layer)
+    gains, shifts = gain_rows.at[0], shift_rows.at[0]
+
+    def either(first, second):
+        return jnp.where(copy == 0, first, second)
 
     def at(position):
         far = position >= line
@@ -82,17 +89,81 @@
         return lax.rem(position + 2 * chips, chips)
 
     across = (1 - section, copy, dp)
+    beside = (section, 1 - copy, dp)
     sibling = (section, copy, dp + 1 - 2 * core)
     ahead, behind = at(around(place + 1)), at(around(place - 1))
 
+    def load(unit):
+        group, odd = unit // 2, unit % 2
+        if odd:
+            source, target, size = either(shift, 0), either(0, REACH), rows - REACH
+        else:
+            source, target, size = either(0, local - rows), 0, rows
+        return pltpu.make_async_copy(
+            boundary.at[0, group, 0, pl.ds(pl.multiple_of(source, 16), size)],
+            xb.at[0, pl.ds(pl.multiple_of(unit * rows + target, 16), size)], in_sem.at[unit],
+        )
+
+    def halo(group):
+        source, target = either(local - REACH, 0), (2 * group + 1) * rows + either(0, rows - REACH)
+        return pltpu.make_async_remote_copy(
+            src_ref=boundary.at[0, group, 0, pl.ds(pl.multiple_of(source, 16), REACH)],
+            dst_ref=xb.at[0, pl.ds(pl.multiple_of(target, 16), REACH)],
+            send_sem=y_send.at[group], recv_sem=y_recv.at[group],
+            device_id=beside, device_id_type=MESH,
+        )
+
+    weights = [
+        pltpu.make_async_copy(source.at[0], target, weight_sem.at[index])
+        for index, (source, target) in enumerate(
+            ((qkv_weight, w_qkv), (out_weight, w_out), (inner_weight, w_in), (outer_weight, w_outer))
+        )
+    ]
     vec[...] = jnp.zeros_like(vec)
     barrier = pltpu.get_barrier_semaphore()
-    for other in (across, sibling, ahead, behind):
+    for other in (across, beside, sibling, ahead, behind):
         pl.semaphore_signal(barrier, inc=1, device_id=other, device_id_type=MESH)
-    load = pltpu.make_async_copy(given, xb.at[0], in_sem)
-    load.start()
-    load.wait()
-    pl.semaphore_wait(barrier, 4)
+    load(0).start()
+    weights[0].start()
+    for unit in range(1, units):
+        load(unit).start()
+    for weight in weights[1:]:
+        weight.start()
+
+    spot = lax.broadcasted_iota(jnp.int32, (micro, length), 1)
+    sentence = ids[:, 0, :]
+    cuts = (reach // 2, local, length - reach // 2)
+    owner = jnp.zeros((micro, length), jnp.int32)
+    for cut in cuts:
+        owner = owner + jnp.where(spot >= cut, 1, 0)
+    for index, cut in enumerate(cuts):
+        crossing = sentence == sentence[:, cut - 1 : cut]
+        left = jnp.sum(jnp.where(crossing & (spot < cut), 1.0, 0.0), axis=1, keepdims=True)
+        right = jnp.sum(jnp.where(crossing & (spot >= cut), 1.0, 0.0), axis=1, keepdims=True)
+        side = jnp.where(left >= right, index, index + 1)
+        owner = jnp.where(crossing, side, owner)
+    info[...] = jnp.zeros_like(info)
+    info[0:micro] = sentence.astype(F32)
+    info[micro : 2 * micro] = owner.astype(F32)
+    column[...] = info[...].T
+
+    def piece_of(unit):
+        odd = lax.rem(unit, 2)
+        return either(odd, 1 - odd)
+
+    def begin_of(unit):
+        return copy * (local - REACH) + piece_of(unit) * shift
+
+    def pick(unit, first, size, kind):
+        spots = pl.ds(pl.multiple_of(begin_of(unit) + first, 16), size)
+        both = column[spots, kind * micro : (kind + 1) * micro]
+        return jnp.where(unit < 2, both[:, 0:1], both[:, 1:2])
+
+    def owned(unit, first, size):
+        return pick(unit, first, size, 1) == (2 * copy + piece_of(unit)).astype(F32)
+
+    load(0).wait()
+    weights[0].wait()
 
     def unit_rows(unit):
         return pl.ds(pl.multiple_of(unit * rows, 16), rows)
@@ -104,7 +175,7 @@
             recv_sem=x_recv.at[unit], device_id=across, device_id_type=MESH,
         )
 
-    def forward(unit):
+    def forward(unit, slot):
         span = unit_rows(unit)
         start = pl.multiple_of(unit * rows, 16)
         hidden = xb[section, span]
@@ -112,7 +183,9 @@
         lane = lax.broadcasted_iota(jnp.int32, scaled_qkv.shape, 1)
         mixed[span] = jnp.where(lane < width, scaled_qkv * 0.125, scaled_qkv).astype(BF16)
         for index, (first, size, begin) in enumerate(blocks):
-            allowed = id_col[unit, first : first + size] == id_row[unit, index : index + 1]
+            turned = pltpu.roll(info[0:8], length - begin_of(unit) - begin, 1)[0:micro, 0:WINDOW]
+            near_ids = jnp.where(unit < 2, turned[0:1], turned[1:2])
+            allowed = pick(unit, first, size, 0) == near_ids
             bias[first : first + size] = jnp.where(allowed, 0.0, NEG)
 
         def pair_step(pair, _):
@@ -123,18 +196,31 @@
                 query = mixed[own, pl.ds(lanes, 128)]
                 keys = halves(mixed[near, pl.ds(pl.multiple_of(width + pair * 128, 128), 128)])
                 values = halves(mixed[near, pl.ds(pl.multiple_of(2 * width + pair * 128, 128), 128)])
+                ones = halves(jnp.ones((WINDOW, 128), BF16))
                 shares = []
                 for head in range(2):
                     scores = against(query, keys[head]) + bias[first : first + size]
-                    weights = jnp.exp(scores - jnp.max(scores, axis=-1, keepdims=True))
-                    share = (weights * (1.0 / jnp.sum(weights, axis=-1, keepdims=True))).astype(BF16)
+                    share = jnp.exp(scores - jnp.max(scores, axis=-1, keepdims=True)).astype(BF16)
                     probs[own, pl.ds(pl.multiple_of(pair * 512 + head * 256, 256), 256)] = share
                     shares.append(share)
-                attended = mul(jnp.concatenate(shares, axis=1), jnp.concatenate(values, axis=0))
-                att[own, pl.ds(lanes, 128)] = attended.astype(BF16)
+                sides = [jnp.concatenate([values[head], ones[head]], axis=1) for head in range(2)]
+                sums = mul(jnp.concatenate(shares, axis=1), jnp.concatenate(sides, axis=0))
+                inverse = 1.0 / sums[:, 128:]
+                att[own, pl.ds(lanes, 128)] = (sums[:, :128] * inverse).astype(BF16)
+                scale[own, pl.ds(lanes, 128)] = inverse
             return 0
 
-        lax.fori_loop(0, width // 128, pair_step, 0)
+        lax.fori_loop(0, width // 128, pair_step, 0, unroll=True)
+        @pl.when(slot == 0)
+        def _():
+            for weight in weights[1:]:
+                weight.wait()
+            for odd in range(1, units):
+                load(odd).wait()
+            pl.semaphore_wait(barrier, 5)
+            for group in range(micro):
+                halo(group).start()
+
         scaled, inverse = normalize(xb[section, span].astype(F32) + mul(att[span], w_out[...]))
         one[span] = scaled
         inv_one[span] = inverse
@@ -164,7 +250,7 @@
     def backward(unit):
         span = unit_rows(unit)
         start = pl.multiple_of(unit * rows, 16)
-        upstream = xb[1 - section, span].astype(F32) * valid[unit]
+        upstream = jnp.where(owned(unit, 0, rows), xb[1 - section, span].astype(F32), 0.0)
         scaled = two[span]
         vec[1:2] += jnp.sum(upstream * scaled, axis=0, keepdims=True)
         vec[3:4] += jnp.sum(upstream, axis=0, keepdims=True)
@@ -191,7 +277,7 @@
         hold[...] = grad_one
         low = grad_one.astype(BF16)
         gai[span] = low
-        gatt[...] = against(low, w_out[...]).astype(BF16)
+        gatt[...] = (against(low, w_out[...]) * scale[span]).astype(BF16)
 
         def pair_step(pair, _):
             lanes = pl.multiple_of(pair * 128, 128)
@@ -204,41 +290,48 @@
                 queries = halves(mixed[own, pl.ds(lanes, 128)])
                 keys = halves(mixed[near, key_lanes])
                 values = halves(mixed[near, value_lanes])
+                minus = halves(jnp.full((WINDOW, 128), -1.0, BF16))
                 grad_pair = gatt[first : first + size, pl.ds(lanes, 128)]
+                paired = (grad_pair.astype(F32) * att[own, pl.ds(lanes, 128)].astype(F32)).astype(BF16)
+                left = jnp.concatenate([grad_pair, paired], axis=1)
                 shares, grads = [], []
                 for head in range(2):
                     share = probs[own, pl.ds(pl.multiple_of(pair * 512 + head * 256, 256), 256)]
-                    wide = share.astype(F32)
-                    grad_probs = against(grad_pair, values[head])
-                    rowwise = jnp.sum(wide * grad_probs, axis=-1, keepdims=True)
-                    grads.append((wide * (grad_probs - rowwise)).astype(BF16))
+                    tilt = against(left, jnp.concatenate([values[head], minus[head]], axis=1))
+                    grads.append((share.astype(F32) * tilt).astype(BF16))
                     shares.append(share)
                 grad_query = mul(jnp.concatenate(grads, axis=1), jnp.concatenate(keys, axis=0))
                 gmix[own, pl.ds(lanes, 128)] = (grad_query * 0.125).astype(BF16)
-                dkv[0, begin : begin + WINDOW] += contract(
-                    jnp.concatenate(grads, axis=0), jnp.concatenate(queries, axis=0)
+                grad_key = contract(jnp.concatenate(queries, axis=0), jnp.concatenate(grads, axis=0))
+                grad_value = contract(
+                    jnp.concatenate(halves(grad_pair), axis=0), jnp.concatenate(shares, axis=0)
                 )
-                dkv[1, begin : begin + WINDOW] += contract(
-                    jnp.concatenate(shares, axis=0), jnp.concatenate(halves(grad_pair), axis=0)
-                )
+                dkv[0, begin : begin + WINDOW] += grad_key.T
+                dkv[1, begin : begin + WINDOW] += grad_value.T
             gmix[span, key_lanes] = dkv[0].astype(BF16)
             gmix[span, value_lanes] = dkv[1].astype(BF16)
             return 0
 
-        lax.fori_loop(0, width // 128, pair_step, 0)
+        lax.fori_loop(0, width // 128, pair_step, 0, unroll=True)
         ob[1 - section, span] = (hold[...] + against(gmix[span], w_qkv[...])).astype(BF16)
 
     def slot_step(slot, _):
         is_forward = jnp.where(section == 0, slot < units, lax.rem(slot, 2) == 0)
         unit = jnp.where(section == 0, lax.rem(slot, units), lax.div(slot, 2))
 
+        first_use = jnp.where(section == 0, is_forward, jnp.logical_not(is_forward))
+
+        @pl.when(jnp.logical_and(first_use, lax.rem(unit, 2) == 1))
+        def _():
+            halo(lax.div(unit, 2)).wait_recv()
+
         @pl.when(is_forward)
         def _():
             @pl.when(section == 1)
             def _():
                 x_copy(unit).wait_recv()
 
-            forward(unit)
+            forward(unit, slot)
 
             @pl.when(section == 0)
             def _():
@@ -259,8 +352,50 @@
         return 0
 
     lax.fori_loop(0, 2 * units, slot_step, 0)
-    write = pltpu.make_async_copy(ob.at[1], result, out_sem)
-    write.start()
+
+    def strip_copy(group):
+        source = (2 * group + 1) * rows + either(rows - REACH, 0)
+        return pltpu.make_async_remote_copy(
+            src_ref=ob.at[1, pl.ds(pl.multiple_of(source, 16), REACH)], dst_ref=strip.at[group],
+            send_sem=y_send.at[micro + group], recv_sem=y_recv.at[micro + group],
+            device_id=beside, device_id_type=MESH,
+        )
+
+    def outputs(group, side):
+        even, odd = 2 * group * rows, (2 * group + 1) * rows
+        if side == 0:
+            parts = ((even, 0, shift), (odd, shift, local - shift))
+        else:
+            parts = ((odd + REACH, 0, shift - REACH), (even, shift - REACH, rows))
+        return [
+            pltpu.make_async_copy(
+                ob.at[1, pl.ds(source, size)], result.at[0, group, 0, pl.ds(target, size)],
+                out_sem.at[group, index],
+            )
+            for index, (source, target, size) in enumerate(parts)
+        ]
+
+    for group in range(micro):
+        strip_copy(group).start()
+
+    def finish():
+        for group in range(micro):
+            low_unit, high_unit = 2 * group + copy, 2 * group + 1 - copy
+            over = rows - shift
+            kept = pl.ds(pl.multiple_of(low_unit * rows + shift, 16), over)
+            moved = pl.ds(pl.multiple_of(high_unit * rows, 16), over)
+            ob[1, moved] = jnp.where(owned(low_unit, shift, over), ob[1, kept], ob[1, moved])
+            strip_copy(group).wait_recv()
+            odd_unit = 2 * group + 1
+            first = either(shift, REACH)
+            edge = pl.ds(pl.multiple_of(odd_unit * rows + first, 16), REACH)
+            ob[1, edge] = jnp.where(owned(odd_unit, first, REACH), ob[1, edge], strip[group])
+        for side in range(2):
+            @pl.when(copy == side)
+            def _():
+                for group in range(micro):
+                    for part in outputs(group, side):
+                        part.start()
 
     half = 1024
     seg = half // chips
@@ -411,6 +546,7 @@
         copy_of.start()
     joined(1)
     joined(2)
+    finish()
     vec_copy.wait()
     slots[0] = vec[0:8] + vec[8:16]
 
@@ -479,7 +615,39 @@
         return 0
 
     lax.fori_loop(0, units, drain_units, 0)
-    write.wait()
+    for group in range(micro):
+        halo(group).wait_send()
+        strip_copy(group).wait_send()
+    for side in range(2):
+        @pl.when(copy == side)
+        def _():
+            for group in range(micro):
+                for part in outputs(group, side):
+                    part.wait()
+
+
+def widen(summed, vectors, qkv, out, inner, outer, gain, shift):
+    step = pl.program_id(0)
+    wide = jnp.concatenate([summed[0, 0], summed[0, 1]], axis=1).astype(F32)
+
+    @pl.when(step < 4)
+    def _():
+        outer[0] = wide
+
+    @pl.when(jnp.logical_and(step >= 4, step < 8))
+    def _():
+        inner[0] = wide
+
+    @pl.when(step == 8)
+    def _():
+        out[0] = wide
+
+    @pl.when(step > 8)
+    def _():
+        qkv[0] = wide
+
+    gain[0] = vectors[0:2]
+    shift[0] = vectors[2:4]
 
 
 def per_device(mesh, boundary, sentence_ids, qkv_weight, out_weight, inner_weight, outer_weight, norm_gain, norm_bias):
@@ -487,45 +655,9 @@
     inner_width = inner_weight.shape[2]
     length = sentence_ids.shape[2]
     chips = mesh.shape["copy"] * mesh.shape["dp"] // 2
-    copy = lax.axis_index("copy")
-    reach = local + REACH
-    pieces = PIECES
-    rows = reach if pieces == 1 else reach // 2 + REACH
-    begins = (0,) if pieces == 1 else (0, reach - rows)
-    units = micro * pieces
+    rows = (local + REACH) // 2 + REACH
+    units = micro * 2
     tokens = units * rows
-    own = boundary[0, :, 0]
-    ids = sentence_ids[:, 0]
-
-    def swap(strip):
-        return lax.ppermute(strip, "copy", [(0, 1), (1, 0)])
-
-    def split(whole):
-        return jnp.stack([whole[m, b : b + rows] for m in range(micro) for b in begins])
-
-    strip = lax.dynamic_slice_in_dim(own, (1 - copy) * (local - REACH), REACH, 1)
-    strip = swap(strip)
-    reaching = jnp.where(
-        copy == 0, jnp.concatenate([own, strip], axis=1), jnp.concatenate([strip, own], axis=1)
-    )
-    given = split(reaching).reshape(tokens, width)
-    start = copy * (local - REACH)
-    near_ids = lax.dynamic_slice_in_dim(ids, start, reach, 1)
-    unit_ids = split(near_ids)
-    cuts = (local,) if pieces == 1 else (reach // 2, local, length - reach // 2)
-    spot = jnp.arange(length)
-    owner = sum((spot >= cut).astype(jnp.int32) for cut in cuts)[None]
-    for index, cut in enumerate(cuts):
-        crossing = ids == ids[:, cut - 1 : cut]
-        left = jnp.sum(crossing & (spot < cut), axis=1, keepdims=True)
-        right = jnp.sum(crossing & (spot >= cut), axis=1, keepdims=True)
-        owner = jnp.where(crossing, jnp.where(left >= right, index, index + 1), owner)
-    near_owner = lax.dynamic_slice_in_dim(owner, start, reach, 1) - copy * pieces
-    valid = jnp.stack(
-        [near_owner[m, b : b + rows] == j for m in range(micro) for j, b in enumerate(begins)]
-    )
-    id_row = jnp.stack([unit_ids[:, b : b + WINDOW] for _, _, b in BLOCKS[pieces]], axis=1)
-
     any_space = pl.BlockSpec(memory_space=pl.ANY)
     vmem = pl.BlockSpec(memory_space=pltpu.VMEM)
     dma = pltpu.SemaphoreType.DMA
@@ -533,13 +665,19 @@
     result, summed, vectors = pl.pallas_call(
         functools.partial(kernel, units, rows, chips, width, inner_width),
         out_shape=(
-            jax.ShapeDtypeStruct((tokens, width), BF16),
+            jax.ShapeDtypeStruct(boundary.shape, BF16),
             jax.ShapeDtypeStruct((GROUPS, 2, 2048, 256), BF16),
             jax.ShapeDtypeStruct((8, width), F32),
         ),
-        in_specs=[any_space] + [vmem] * 9,
+        in_specs=[any_space, vmem] + [any_space] * 4 + [vmem] * 2,
         out_specs=(any_space, any_space, vmem),
         scratch_shapes=[
+            pltpu.VMEM((width, 3 * width), BF16),
+            pltpu.VMEM((width, width), BF16),
+            pltpu.VMEM((width, inner_width), BF16),
+            pltpu.VMEM((inner_width, width), BF16),
+            pltpu.VMEM((128, length), F32),
+            pltpu.VMEM((length, 128), F32),
             pltpu.VMEM((2, tokens, width), BF16),
             pltpu.VMEM((2, tokens, width), BF16),
             pltpu.VMEM((tokens, 3 * width), BF16),
@@ -555,56 +693,51 @@
             pltpu.VMEM((tokens, width), BF16),
             pltpu.VMEM((tokens, 3 * width), BF16),
             pltpu.VMEM((tokens, HEADS * WINDOW), BF16),
+            pltpu.VMEM((tokens, width), F32),
             pltpu.VMEM((rows, WINDOW), F32),
             pltpu.VMEM((rows, width), BF16),
             pltpu.VMEM((rows, width), F32),
             pltpu.VMEM((2, rows, 128), F32),
+            pltpu.VMEM((micro, REACH, width), BF16),
             pltpu.VMEM((GROUPS, 2, 1024, 256), BF16),
             pltpu.VMEM((GROUPS, 2, 1024, 256), BF16),
             pltpu.VMEM((GROUPS, 2, hops, 1024 // chips, 256), BF16),
             pltpu.VMEM((16, width), F32),
             pltpu.VMEM((chips, 8, width), F32),
-            dma, dma, dma((units,)), dma((units,)), dma((GROUPS, 2)), dma((GROUPS, 2)),
+            dma((4,)), dma((units,)), dma((micro, 2)), dma((units,)), dma((units,)),
+            dma((2 * micro,)), dma((2 * micro,)), dma((GROUPS, 2)), dma((GROUPS, 2)),
             dma((GROUPS, 2, hops)), dma((GROUPS, 2, hops)), dma((GROUPS, 2, hops)), dma((GROUPS, 2, hops)),
             dma((chips + 1,)), dma((chips + 1,)), dma((GROUPS, 2)), dma((GROUPS, 2)), dma((GROUPS, 2)),
         ],
         compiler_params=pltpu.CompilerParams(
             collective_id=0, has_side_effects=True, vmem_limit_bytes=63 * 1024 * 1024
         ),
-    )(
-        given, unit_ids[:, :, None], id_row, valid[:, :, None].astype(F32),
-        qkv_weight[0], out_weight[0], inner_weight[0], outer_weight[0], norm_gain[0], norm_bias[0],
-    )
-
-    parts = result.reshape(micro, pieces, rows, width)
-    valid = valid.reshape(micro, pieces, rows, 1)
-    merged, merged_valid = parts[:, 0], valid[:, 0]
-    if pieces == 2:
-        cut = begins[1]
-        over = rows - cut
-        blend = jnp.where(valid[:, 0, cut:], parts[:, 0, cut:], parts[:, 1, :over])
-        merged = jnp.concatenate([parts[:, 0, :cut], blend, parts[:, 1, over:]], axis=1)
-        merged_valid = jnp.concatenate(
-            [valid[:, 0, :cut], valid[:, 0, cut:] | valid[:, 1, :over], valid[:, 1, over:]], axis=1
-        )
-    strip = swap(lax.dynamic_slice_in_dim(merged, (1 - copy) * local, REACH, 1))
-    final = lax.dynamic_slice_in_dim(merged, copy * REACH, local, 1)
-    final_valid = lax.dynamic_slice_in_dim(merged_valid, copy * REACH, local, 1)
-    edge = (1 - copy) * (local - REACH)
-    kept = jnp.where(
-        lax.dynamic_slice_in_dim(final_valid, edge, REACH, 1),
-        lax.dynamic_slice_in_dim(final, edge, REACH, 1), strip,
-    )
-    final = lax.dynamic_update_slice_in_dim(final, kept, edge, 1)
-
-    wide = summed.astype(F32)
-    joined = jnp.concatenate([wide[:, 0], wide[:, 1]], axis=-1)
-    grad_inner = joined[1].reshape(4, 512, 512).transpose(1, 0, 2).reshape(width, inner_width)
-    grad_qkv = joined[2, 512:].reshape(3, 512, 512).transpose(1, 0, 2).reshape(width, 3 * width)
-    return (
-        final[None, :, None], grad_qkv[None], joined[2, :512][None], grad_inner[None], joined[0][None],
-        vectors[None, 0:2], vectors[None, 2:4],
-    )
+    )(boundary, sentence_ids, qkv_weight, out_weight, inner_weight, outer_weight, norm_gain, norm_bias)
+
+    def block(low, count, column):
+        def index(step):
+            spot = jnp.clip(step - low, 0, count - 1)
+            return (0, 0, spot) if column else (0, spot, 0)
+
+        return pl.BlockSpec((1, 512, 512), index)
+
+    vector = pl.BlockSpec((1, 2, width), lambda step: (0, 0, 0))
+    grad_qkv, grad_out, grad_inner, grad_outer, grad_gain, grad_bias = pl.pallas_call(
+        widen,
+        grid=(4 * GROUPS,),
+        out_shape=tuple(
+            jax.ShapeDtypeStruct(item.shape, F32)
+            for item in (qkv_weight, out_weight, inner_weight, outer_weight, norm_gain, norm_bias)
+        ),
+        in_specs=[
+            pl.BlockSpec((1, 2, 512, 256), lambda step: (step // 4, 0, step % 4, 0)),
+            pl.BlockSpec((8, width), lambda step: (0, 0)),
+        ],
+        out_specs=(
+            block(9, 3, True), block(8, 1, True), block(4, 4, True), block(0, 4, False), vector, vector,
+        ),
+    )(summed, vectors)
+    return (result, grad_qkv, grad_out, grad_inner, grad_outer, grad_gain, grad_bias)
 
 
 def solution(mesh):

time: 229 us -> 166 us (0.72)
  local copies, waits for them, and re-layouts: 30.9 us -> 0.97 us
  other arithmetic: 21.7 us -> 0 us
  Pallas kernels: 171 us -> 164 us
  starting transfers between devices: 4.14 us -> 0 us
    pallas_call x1, Pallas kernels: 171 us -> 152 us  [per_device(): pl.pallas_call(functools.partial(kernel, units, rows, chips, width, inner...]
    pallas_call x0 -> x1, Pallas kernels: none -> 12 us  [per_device(): pl.pallas_call(widen, grid=(4 * GROUPS,), out_shape=tuple((jax.ShapeDtype...]
    convert_element_type x2 -> x0, other arithmetic: 9.39 us -> none  [the longest x1 8.5 us: per_device(): wide = summed.astype(F32)]
    another operation x9 -> x0, local copies, waits for them, and re-layouts: 9.24 us -> none  [the longest x1 6.05 us: per_device(): grad_inner[None]]
    squeeze x2 -> x0, local copies, waits for them, and re-layouts: 8.62 us -> none  [the longest x1 8.56 us: per_device(): joined = jnp.concatenate([wide[:, 0], wide[:, 1]], axis=-1)]
    concatenate x4 -> x0, other arithmetic: 7.29 us -> none  [the longest x3 7.21 us: per_device(): joined = jnp.concatenate([wide[:, 0], wide[:, 1]], axis=-1)]
    transpose x1 -> x0, local copies, waits for them, and re-layouts: 4.62 us -> none  [per_device(): joined[1].reshape(4, 512, 512).transpose(1, 0, 2)]
    ppermute x2 -> x0, starting transfers between devices: 4.14 us -> none  [swap(): return lax.ppermute(strip, 'copy', [(0, 1), (1, 0)])]
  transfers between devices with their start and end apart: 2 -> 0, of which waited for: 0 -> 0; matrix products, arithmetic and copies ran while one was open for 10% -> 0% of each run, Pallas kernels for 0% -> 0%
where the time goes in v1:
time: 166 us
  Pallas kernels  164 us (99%)
    pallas_call x1, Pallas kernels, per_device(): pl.pallas_call(functools.partial(kernel, units, rows, chips, width, inner...  152 us
    pallas_call x1, Pallas kernels, per_device(): pl.pallas_call(widen, grid=(4 * GROUPS,), out_shape=tuple((jax.ShapeDtype...  12 us

profile of v1, /device:TPU:0, one launch (start us, length us, event | category | flops | bytes accessed | tf_op | source)
XLA Modules:
  0.0 165.7 jit_solution(1524261861382120334)
XLA Ops:
  0.6 152.1 %shard_map.135 = (bf16[1,2,1,512,512]{4,3,2,1,0:T(8,128)(2,1)}, bf16[3,2,2048,256]{3,2,1,0:T(8,128)(2,1)}, f32[8,512]{1,0:T(8,128)}) custom-call(bf16[1,2,1,512,512]{4,3,2,1,0:T(8,128)(2,1)} %boundary.1, s32[2,1,1024]{2,1,0:T(1,128)} %ids.1, bf16[1,512,1536]{2,1,0:T(8,128)(2,1)} %qkv_weight.1, bf16[1,512,512]{2,1,0:T(8,128)(2,1)} %out_weight.1, ...), custom_call_target="tpu_custom_call" | custom-call | tf_op jit(solution)/shard_map/pallas_call | solution.py:665
  152.8 0.0 copy-start
  152.8 12.0 %shard_map.136 = (f32[1,512,1536]{2,1,0:T(8,128)}, f32[1,512,512]{2,1,0:T(8,128)}, f32[1,512,2048]{2,1,0:T(8,128)}, f32[1,2048,512]{2,1,0:T(8,128)}, f32[1,2,512]{2,1,0:T(2,128)}, /*index=5*/f32[1,2,512]{2,1,0:T(2,128)}) custom-call(bf16[3,2,2048,256]{3,2,1,0:T(8,128)(2,1)} %get-tuple-element.17.summed, f32[8,512]{1,0:T(8,128)} %get-tuple-element.18.vectors), custom_call_target="tpu_custom_call" | custom-call | tf_op jit(solution)/shard_map/pallas_call | solution.py:725
  164.8 0.0 copy-done
  164.8 1.0 copy.16
Async XLA Ops:
  152.8 12.0 %copy-start = (bf16[1,2,1,512,512]{4,3,2,1,0:T(8,128)(2,1)S(1)}, bf16[1,2,1,512,512]{4,3,2,1,0:T(8,128)(2,1)}, u32[]{:S(2)}) copy-start(bf16[1,2,1,512,512]{4,3,2,1,0:T(8,128)(2,1)} %get-tuple-element.32) | copy-start | bytes 3145732

commit v2 on v1

--- a/solution.py
+++ b/solution.py
@@ -13,7 +13,7 @@
 NEG = -1e30
 EPS = 1e-05
 GROUPS = 3
-BLOCKS = ((0, 160, 0), (160, 144, 48))
+BLOCKS = ((0, 192, 0), (192, 112, 128))
 MESH = pl.DeviceIdType.MESH
 F32 = jnp.float32
 BF16 = jnp.bfloat16
@@ -120,6 +120,7 @@
         )
     ]
     vec[...] = jnp.zeros_like(vec)
+    mixed[...] = jnp.zeros_like(mixed)
     barrier = pltpu.get_barrier_semaphore()
     for other in (across, beside, sibling, ahead, behind):
         pl.semaphore_signal(barrier, inc=1, device_id=other, device_id_type=MESH)
@@ -185,6 +186,8 @@
         for index, (first, size, begin) in enumerate(blocks):
             turned = pltpu.roll(info[0:8], length - begin_of(unit) - begin, 1)[0:micro, 0:WINDOW]
             near_ids = jnp.where(unit < 2, turned[0:1], turned[1:2])
+            inside = lax.broadcasted_iota(jnp.int32, near_ids.shape, 1) < rows - begin
+            near_ids = jnp.where(inside, near_ids, -1.0)
             allowed = pick(unit, first, size, 0) == near_ids
             bias[first : first + size] = jnp.where(allowed, 0.0, NEG)
 
@@ -193,20 +196,20 @@
             for first, size, begin in blocks:
                 near = pl.ds(pl.multiple_of(start + begin, 16), WINDOW)
                 own = pl.ds(pl.multiple_of(start + first, 16), size)
-                query = mixed[own, pl.ds(lanes, 128)]
-                keys = halves(mixed[near, pl.ds(pl.multiple_of(width + pair * 128, 128), 128)])
-                values = halves(mixed[near, pl.ds(pl.multiple_of(2 * width + pair * 128, 128), 128)])
-                ones = halves(jnp.ones((WINDOW, 128), BF16))
-                shares = []
+                query = jnp.concatenate(halves(mixed[own, pl.ds(lanes, 128)]), axis=0)
+                key = mixed[near, pl.ds(pl.multiple_of(width + pair * 128, 128), 128)]
+                value = mixed[near, pl.ds(pl.multiple_of(2 * width + pair * 128, 128), 128)]
+                barred = bias[first : first + size]
+                scores = against(query, key) + jnp.concatenate([barred, barred], axis=0)
+                share = jnp.exp(scores - jnp.max(scores, axis=-1, keepdims=True)).astype(BF16)
                 for head in range(2):
-                    scores = against(query, keys[head]) + bias[first : first + size]
-                    share = jnp.exp(scores - jnp.max(scores, axis=-1, keepdims=True)).astype(BF16)
-                    probs[own, pl.ds(pl.multiple_of(pair * 512 + head * 256, 256), 256)] = share
-                    shares.append(share)
-                sides = [jnp.concatenate([values[head], ones[head]], axis=1) for head in range(2)]
-                sums = mul(jnp.concatenate(shares, axis=1), jnp.concatenate(sides, axis=0))
-                inverse = 1.0 / sums[:, 128:]
-                att[own, pl.ds(lanes, 128)] = (sums[:, :128] * inverse).astype(BF16)
+                    cols = pl.ds(pl.multiple_of(pair * 512 + head * 256, 256), 256)
+                    probs[own, cols] = share[head * size : (head + 1) * size]
+                sums = mul(share, jnp.concatenate([value, jnp.ones((WINDOW, 128), BF16)], axis=1))
+                lane = lax.broadcasted_iota(jnp.int32, (size, 128), 1)
+                inverse = 1.0 / jnp.where(lane < 64, sums[:size, 128:], sums[size:, 128:])
+                attended = jnp.where(lane < 64, sums[:size, :128], sums[size:, :128])
+                att[own, pl.ds(lanes, 128)] = (attended * inverse).astype(BF16)
                 scale[own, pl.ds(lanes, 128)] = inverse
             return 0
 
@@ -247,9 +250,8 @@
         inv_two[span] = inverse
         ob[section, span] = (scaled * gains[1:2] + shifts[1:2]).astype(BF16)
 
-    def backward(unit):
+    def backward_norm(unit):
         span = unit_rows(unit)
-        start = pl.multiple_of(unit * rows, 16)
         upstream = jnp.where(owned(unit, 0, rows), xb[1 - section, span].astype(F32), 0.0)
         scaled = two[span]
         vec[1:2] += jnp.sum(upstream * scaled, axis=0, keepdims=True)
@@ -257,6 +259,9 @@
         grad_two = normalize_back(upstream, scaled, inv_two[span], gains[1:2])
         hold[...] = grad_two
         goi[span] = grad_two.astype(BF16)
+
+    def backward_feed(unit):
+        span = unit_rows(unit)
         tile = 512
         count = inner_width // tile
         grad_active = against(goi[span], w_outer[0:tile])
@@ -270,6 +275,12 @@
             dg[span, cols] = grad_inner
             total = total + against(grad_inner, w_in[:, step * tile : (step + 1) * tile])
             grad_active = next_active
+        hold[...] = total
+
+    def backward_rest(unit):
+        span = unit_rows(unit)
+        start = pl.multiple_of(unit * rows, 16)
+        total = hold[...]
         scaled = one[span]
         vec[0:1] += jnp.sum(total * scaled, axis=0, keepdims=True)
         vec[2:3] += jnp.sum(total, axis=0, keepdims=True)
@@ -287,33 +298,41 @@
             for first, size, begin in blocks:
                 near = pl.ds(pl.multiple_of(start + begin, 16), WINDOW)
                 own = pl.ds(pl.multiple_of(start + first, 16), size)
-                queries = halves(mixed[own, pl.ds(lanes, 128)])
-                keys = halves(mixed[near, key_lanes])
-                values = halves(mixed[near, value_lanes])
-                minus = halves(jnp.full((WINDOW, 128), -1.0, BF16))
+                query = jnp.concatenate(halves(mixed[own, pl.ds(lanes, 128)]), axis=0)
+                key = mixed[near, key_lanes]
+                value = mixed[near, value_lanes]
                 grad_pair = gatt[first : first + size, pl.ds(lanes, 128)]
                 paired = (grad_pair.astype(F32) * att[own, pl.ds(lanes, 128)].astype(F32)).astype(BF16)
-                left = jnp.concatenate([grad_pair, paired], axis=1)
-                shares, grads = [], []
-                for head in range(2):
-                    share = probs[own, pl.ds(pl.multiple_of(pair * 512 + head * 256, 256), 256)]
-                    tilt = against(left, jnp.concatenate([values[head], minus[head]], axis=1))
-                    grads.append((share.astype(F32) * tilt).astype(BF16))
-                    shares.append(share)
-                grad_query = mul(jnp.concatenate(grads, axis=1), jnp.concatenate(keys, axis=0))
+                grad = jnp.concatenate(halves(grad_pair), axis=0)
+                left = jnp.concatenate([grad, jnp.concatenate(halves(paired), axis=0)], axis=1)
+                share = jnp.concatenate(
+                    [probs[own, pl.ds(pl.multiple_of(pair * 512 + head * 256, 256), 256)] for head in range(2)],
+                    axis=0,
+                )
+                tilt = against(left, jnp.concatenate([value, jnp.full((WINDOW, 128), -1.0, BF16)], axis=1))
+                grads = (share.astype(F32) * tilt).astype(BF16)
+                wide = mul(grads, key)
+                lane = lax.broadcasted_iota(jnp.int32, (size, 128), 1)
+                grad_query = jnp.where(lane < 64, wide[:size], wide[size:])
                 gmix[own, pl.ds(lanes, 128)] = (grad_query * 0.125).astype(BF16)
-                grad_key = contract(jnp.concatenate(queries, axis=0), jnp.concatenate(grads, axis=0))
-                grad_value = contract(
-                    jnp.concatenate(halves(grad_pair), axis=0), jnp.concatenate(shares, axis=0)
-                )
-                dkv[0, begin : begin + WINDOW] += grad_key.T
-                dkv[1, begin : begin + WINDOW] += grad_value.T
-            gmix[span, key_lanes] = dkv[0].astype(BF16)
-            gmix[span, value_lanes] = dkv[1].astype(BF16)
+                for kind, (small, sides) in enumerate(((mixed[own, pl.ds(lanes, 128)], grads), (grad_pair, share))):
+                    turned = small.T
+                    for head in range(2):
+                        heads = slice(head * 64, (head + 1) * 64)
+                        dkv[kind, heads, begin : begin + WINDOW] += mul(
+                            turned[heads], sides[head * size : (head + 1) * size]
+                        )
+            gmix[span, key_lanes] = dkv[0].astype(BF16).T[0:rows]
+            gmix[span, value_lanes] = dkv[1].astype(BF16).T[0:rows]
             return 0
 
         lax.fori_loop(0, width // 128, pair_step, 0, unroll=True)
         ob[1 - section, span] = (hold[...] + against(gmix[span], w_qkv[...])).astype(BF16)
+
+    def backward(unit):
+        backward_norm(unit)
+        backward_feed(unit)
+        backward_rest(unit)
 
     def slot_step(slot, _):
         is_forward = jnp.where(section == 0, slot < units, lax.rem(slot, 2) == 0)
@@ -337,7 +356,9 @@
             def _():
                 x_copy(unit).start()
 
-        @pl.when(jnp.logical_not(is_forward))
+        held = jnp.logical_and(section == 0, slot == 2 * units - 1)
+
+        @pl.when(jnp.logical_not(jnp.logical_or(is_forward, held)))
         def _():
             @pl.when(section == 0)
             def _():
@@ -374,9 +395,6 @@
             )
             for index, (source, target, size) in enumerate(parts)
         ]
-
-    for group in range(micro):
-        strip_copy(group).start()
 
     def finish():
         for group in range(micro):
@@ -400,51 +418,59 @@
     half = 1024
     seg = half // chips
 
-    def sib_copy(group):
-        return [
-            pltpu.make_async_remote_copy(
-                src_ref=probs.at[pl.ds(0, half), pl.ds(pl.multiple_of((group * 2 + way) * 256, 256), 256)],
-                dst_ref=sib.at[group, way], send_sem=sib_send.at[group, way],
-                recv_sem=sib_recv.at[group, way], device_id=sibling, device_id_type=MESH,
-            )
-            for way in range(2)
-        ]
-
-    def keep(group, block, value):
-        value = value.astype(BF16)
-        spot = pl.ds(pl.multiple_of(lax.rem(block, 2) * 512, 512), 512)
-        here = lax.div(block, 2) == core
-
-        @pl.when(here)
-        def _():
+    def spare(group, way, index):
+        tile = way * 2 + index
+        if group == 2:
+            return mixed.at[pl.ds(0, 512), pl.ds(tile * 256, 256)]
+        return probs.at[pl.ds(0, 512), pl.ds((group * 4 + tile) * 256, 256)]
+
+    def sib_copy(group, way, index):
+        return pltpu.make_async_remote_copy(
+            src_ref=spare(group, way, index), dst_ref=sib.at[group, way, pl.ds(index * 512, 512)],
+            send_sem=sib_send.at[group, way, index], recv_sem=sib_recv.at[group, way, index],
+            device_id=sibling, device_id_type=MESH,
+        )
+
+    def block_of(group, block, span):
+        cols = pl.ds(pl.multiple_of(block * 512, 512), 512)
+        if group == 0:
+            return contract(act[span, cols], goi[span])
+        if group == 1:
+            return contract(nlow[span], dg[span, cols])
+        cols = pl.ds(pl.multiple_of(jnp.maximum(block - 1, 0) * 512, 512), 512)
+        left = jnp.where(block == 0, att[span], xb[section, span])
+        return contract(left, jnp.where(block == 0, gai[span], gmix[span, cols]))
+
+    early, late = pl.ds(0, (units - 1) * rows), pl.ds((units - 1) * rows, rows)
+
+    def prepare(group):
+        for index in range(2):
+            value = block_of(group, (1 - core) * 2 + index, early).astype(BF16)
             for way in range(2):
-                mine[group, way, spot] = value[:, way * 256 : (way + 1) * 256]
-
-        @pl.when(jnp.logical_not(here))
-        def _():
+                spare(group, way, index)[...] = value[:, way * 256 : (way + 1) * 256]
+        for index in range(2):
+            value = block_of(group, core * 2 + index, early).astype(BF16)
             for way in range(2):
-                cols = pl.ds((group * 2 + way) * 256, 256)
-                probs[spot, cols] = value[:, way * 256 : (way + 1) * 256]
-
-    def outer_block(block, _):
-        cols = pl.ds(pl.multiple_of(block * 512, 512), 512)
-        keep(0, block, contract(act[:, cols], goi[...]))
-        return 0
-
-    def inner_block(block, _):
-        cols = pl.ds(pl.multiple_of(block * 512, 512), 512)
-        keep(1, block, contract(nlow[...], dg[:, cols]))
-        return 0
-
-    def mixed_block(block, _):
-        cols = pl.ds(pl.multiple_of((block - 1) * 512, 512), 512)
-        keep(2, block, contract(xb[section], gmix[:, cols]))
-        return 0
-
-    def joined(group):
-        for way, copy_of in enumerate(sib_copy(group)):
-            copy_of.wait_recv()
-            mine[group, way] = (mine[group, way].astype(F32) + sib[group, way].astype(F32)).astype(BF16)
+                mine[group, way, index * 512 : (index + 1) * 512] = value[:, way * 256 : (way + 1) * 256]
+
+    def others(group):
+        for index in range(2):
+            value = block_of(group, (1 - core) * 2 + index, late)
+            for way in range(2):
+                part = value[:, way * 256 : (way + 1) * 256]
+                room = spare(group, way, index)
+                room[...] = (room[...].astype(F32) + part).astype(BF16)
+                sib_copy(group, way, index).start()
+
+    def ours(group):
+        for index in range(2):
+            value = block_of(group, core * 2 + index, late)
+            for way in range(2):
+                sib_copy(group, way, index).wait_recv()
+                part = value[:, way * 256 : (way + 1) * 256]
+                span = slice(index * 512, (index + 1) * 512)
+                total = mine[group, way, span].astype(F32) + part + sib[group, way, span].astype(F32)
+                mine[group, way, span] = total.astype(BF16)
 
     def segment(position):
         return pl.ds(pl.multiple_of(around(position) * seg, 16), seg)
@@ -530,22 +556,44 @@
         src_ref=vec.at[pl.ds(0, 8)], dst_ref=vec.at[pl.ds(8, 8)], send_sem=slot_send.at[chips],
         recv_sem=slot_recv.at[chips], device_id=sibling, device_id_type=MESH,
     )
+    def serve(group, step):
+        def each(way, _):
+            ring(group, way, step)
+            return 0
+
+        lax.fori_loop(0, 2, each, 0)
+
+    last = units - 1
+    for group in range(GROUPS):
+        prepare(group)
+
+    @pl.when(section == 0)
+    def _():
+        x_copy(last).wait_recv()
+        backward_norm(last)
+
+    others(0)
+
+    @pl.when(section == 0)
+    def _():
+        backward_feed(last)
+
+    others(1)
+    ours(0)
+    serve(0, 0)
+
+    @pl.when(section == 0)
+    def _():
+        backward_rest(last)
+
+    for group in range(micro):
+        strip_copy(group).start()
     vec_copy.start()
-    lax.fori_loop(0, 4, outer_block, 0)
-    for copy_of in sib_copy(0):
-        copy_of.start()
-    lax.fori_loop(0, 4, inner_block, 0)
-    for copy_of in sib_copy(1):
-        copy_of.start()
-    joined(0)
-    for way in range(2):
-        ring(0, way, 0)
-    keep(2, 0, contract(att[...], gai[...]))
-    lax.fori_loop(1, 4, mixed_block, 0)
-    for copy_of in sib_copy(2):
-        copy_of.start()
-    joined(1)
-    joined(2)
+    others(2)
+    ours(1)
+    serve(1, 0)
+    ours(2)
+    serve(2, 0)
     finish()
     vec_copy.wait()
     slots[0] = vec[0:8] + vec[8:16]
@@ -553,12 +601,7 @@
     def round_step(index, _):
         def each(flat, _):
             group, way = lax.div(flat, 2), lax.rem(flat, 2)
-            step = jnp.where(group == 0, index, index - 1)
-
-            @pl.when(step >= 0)
-            def _():
-                ring(group, way, step)
-
+            ring(group, way, index)
             return 0
 
         lax.fori_loop(0, 2 * GROUPS, each, 0)
@@ -573,7 +616,7 @@
 
         return 0
 
-    lax.fori_loop(1, 2 * chips, round_step, 0)
+    lax.fori_loop(1, 2 * chips - 1, round_step, 0)
     slot_copy(chips - 2).wait_recv()
     total = jnp.zeros((8, width), F32)
     for position in range(chips):
@@ -601,8 +644,9 @@
 
     lax.fori_loop(0, 2 * GROUPS, drain, 0)
     for group in range(GROUPS):
-        for copy_of in sib_copy(group):
-            copy_of.wait_send()
+        for way in range(2):
+            for index in range(2):
+                sib_copy(group, way, index).wait_send()
 
     def drain_slots(step, _):
         slot_copy(step).wait_send()
@@ -626,28 +670,30 @@
                     part.wait()
 
 
-def widen(summed, vectors, qkv, out, inner, outer, gain, shift):
-    step = pl.program_id(0)
-    wide = jnp.concatenate([summed[0, 0], summed[0, 1]], axis=1).astype(F32)
-
-    @pl.when(step < 4)
-    def _():
-        outer[0] = wide
-
-    @pl.when(jnp.logical_and(step >= 4, step < 8))
-    def _():
-        inner[0] = wide
-
-    @pl.when(step == 8)
-    def _():
-        out[0] = wide
-
-    @pl.when(step > 8)
-    def _():
-        qkv[0] = wide
-
+def widen(summed, vectors, qkv, out, inner, outer, gain, shift, narrow, wide, in_sem, out_sem):
+    homes = [outer.at[0, pl.ds(index * 512, 512)] for index in range(4)]
+    homes += [inner.at[0, :, pl.ds(index * 512, 512)] for index in range(4)]
+    homes += [out.at[0]] + [qkv.at[0, :, pl.ds(index * 512, 512)] for index in range(3)]
+    loads = [
+        pltpu.make_async_copy(
+            summed.at[index // 4, :, pl.ds(index % 4 * 512, 512)], narrow.at[index], in_sem.at[index]
+        )
+        for index in range(len(homes))
+    ]
+    stores = [
+        pltpu.make_async_copy(wide.at[index], home, out_sem.at[index]) for index, home in enumerate(homes)
+    ]
+    for load in loads:
+        load.start()
     gain[0] = vectors[0:2]
     shift[0] = vectors[2:4]
+    for index, (load, store) in enumerate(zip(loads, stores)):
+        load.wait()
+        for way in range(2):
+            wide[index, :, way * 256 : (way + 1) * 256] = narrow[index, way].astype(F32)
+        store.start()
+    for store in stores:
+        store.wait()
 
 
 def per_device(mesh, boundary, sentence_ids, qkv_weight, out_weight, inner_weight, outer_weight, norm_gain, norm_bias):
@@ -680,7 +726,7 @@
             pltpu.VMEM((length, 128), F32),
             pltpu.VMEM((2, tokens, width), BF16),
             pltpu.VMEM((2, tokens, width), BF16),
-            pltpu.VMEM((tokens, 3 * width), BF16),
+            pltpu.VMEM((tokens + 80, 3 * width), BF16),
             pltpu.VMEM((tokens, width), BF16),
             pltpu.VMEM((tokens, width), BF16),
             pltpu.VMEM((tokens, inner_width), BF16),
@@ -697,7 +743,7 @@
             pltpu.VMEM((rows, WINDOW), F32),
             pltpu.VMEM((rows, width), BF16),
             pltpu.VMEM((rows, width), F32),
-            pltpu.VMEM((2, rows, 128), F32),
+            pltpu.VMEM((2, 128, 384), F32),
             pltpu.VMEM((micro, REACH, width), BF16),
             pltpu.VMEM((GROUPS, 2, 1024, 256), BF16),
             pltpu.VMEM((GROUPS, 2, 1024, 256), BF16),
@@ -705,7 +751,7 @@
             pltpu.VMEM((16, width), F32),
             pltpu.VMEM((chips, 8, width), F32),
             dma((4,)), dma((units,)), dma((micro, 2)), dma((units,)), dma((units,)),
-            dma((2 * micro,)), dma((2 * micro,)), dma((GROUPS, 2)), dma((GROUPS, 2)),
+            dma((2 * micro,)), dma((2 * micro,)), dma((GROUPS, 2, 2)), dma((GROUPS, 2, 2)),
             dma((GROUPS, 2, hops)), dma((GROUPS, 2, hops)), dma((GROUPS, 2, hops)), dma((GROUPS, 2, hops)),
             dma((chips + 1,)), dma((chips + 1,)), dma((GROUPS, 2)), dma((GROUPS, 2)), dma((GROUPS, 2)),
         ],
@@ -714,28 +760,20 @@
         ),
     )(boundary, sentence_ids, qkv_weight, out_weight, inner_weight, outer_weight, norm_gain, norm_bias)
 
-    def block(low, count, column):
-        def index(step):
-            spot = jnp.clip(step - low, 0, count - 1)
-            return (0, 0, spot) if column else (0, spot, 0)
-
-        return pl.BlockSpec((1, 512, 512), index)
-
-    vector = pl.BlockSpec((1, 2, width), lambda step: (0, 0, 0))
+    blocks = 4 * GROUPS
     grad_qkv, grad_out, grad_inner, grad_outer, grad_gain, grad_bias = pl.pallas_call(
         widen,
-        grid=(4 * GROUPS,),
         out_shape=tuple(
             jax.ShapeDtypeStruct(item.shape, F32)
             for item in (qkv_weight, out_weight, inner_weight, outer_weight, norm_gain, norm_bias)
         ),
-        in_specs=[
-            pl.BlockSpec((1, 2, 512, 256), lambda step: (step // 4, 0, step % 4, 0)),
-            pl.BlockSpec((8, width), lambda step: (0, 0)),
+        in_specs=[any_space, vmem],
+        out_specs=(any_space,) * 4 + (vmem,) * 2,
+        scratch_shapes=[
+            pltpu.VMEM((blocks, 2, 512, 256), BF16), pltpu.VMEM((blocks, 512, 512), F32),
+            dma((blocks,)), dma((blocks,)),
         ],
-        out_specs=(
-            block(9, 3, True), block(8, 1, True), block(4, 4, True), block(0, 4, False), vector, vector,
-        ),
+        compiler_params=pltpu.CompilerParams(vmem_limit_bytes=48 * 1024 * 1024),
     )(summed, vectors)
     return (result, grad_qkv, grad_out, grad_inner, grad_outer, grad_gain, grad_bias)
 

time: 166 us -> 153 us (0.922)
  Pallas kernels: 164 us -> 151 us
    pallas_call x1, Pallas kernels: 152 us -> 144 us  [per_device(): pl.pallas_call(functools.partial(kernel, units, rows, chips, width, inner...]
    pallas_call x1, Pallas kernels: 12 us -> 7.12 us  [per_device(): pl.pallas_call(widen, out_shape=tuple((jax.ShapeDtypeStruct(item.shape, F...]
where the time goes in v2:
time: 153 us
  Pallas kernels  151 us (99%)
  local copies, waits for them, and re-layouts  1.69 us (1%)
    pallas_call x1, Pallas kernels, per_device(): pl.pallas_call(functools.partial(kernel, units, rows, chips, width, inner...  144 us
    pallas_call x1, Pallas kernels, per_device(): pl.pallas_call(widen, out_shape=tuple((jax.ShapeDtypeStruct(item.shape, F...  7.12 us

profile of v2, /device:TPU:0, one launch (start us, length us, event | category | flops | bytes accessed | tf_op | source)
XLA Modules:
  0.0 153.1 jit_solution(8237058924215243315)
XLA Ops:
  0.6 143.6 %shard_map.135 = (bf16[1,2,1,512,512]{4,3,2,1,0:T(8,128)(2,1)}, bf16[3,2,2048,256]{3,2,1,0:T(8,128)(2,1)}, f32[8,512]{1,0:T(8,128)}) custom-call(bf16[1,2,1,512,512]{4,3,2,1,0:T(8,128)(2,1)} %boundary.1, s32[2,1,1024]{2,1,0:T(1,128)} %ids.1, bf16[1,512,1536]{2,1,0:T(8,128)(2,1)} %qkv_weight.1, bf16[1,512,512]{2,1,0:T(8,128)(2,1)} %out_weight.1, ...), custom_call_target="tpu_custom_call" | custom-call | tf_op jit(solution)/shard_map/pallas_call | solution.py:711
  144.2 0.0 copy-start
  144.3 0.7 copy-done
  145.0 0.0 copy-start.1
  145.0 7.1 %shard_map.136 = (f32[1,512,1536]{2,1,0:T(8,128)}, f32[1,512,512]{2,1,0:T(8,128)}, f32[1,512,2048]{2,1,0:T(8,128)}, f32[1,2048,512]{2,1,0:T(8,128)}, f32[1,2,512]{2,1,0:T(2,128)}, /*index=5*/f32[1,2,512]{2,1,0:T(2,128)}) custom-call(bf16[3,2,2048,256]{3,2,1,0:T(8,128)(2,1)} %get-tuple-element.17.summed, f32[8,512]{1,0:T(8,128)S(1)} %copy-done), custom_call_target="tpu_custom_call" | custom-call | tf_op jit(solution)/shard_map/pallas_call | solution.py:764
  152.1 0.0 copy-done.1
  152.1 1.0 copy.16
Async XLA Ops:
  144.2 0.7 copy-start
  145.0 7.1 %copy-start.1 = (bf16[1,2,1,512,512]{4,3,2,1,0:T(8,128)(2,1)S(1)}, bf16[1,2,1,512,512]{4,3,2,1,0:T(8,128)(2,1)}, u32[]{:S(2)}) copy-start(bf16[1,2,1,512,512]{4,3,2,1,0:T(8,128)(2,1)} %get-tuple-element.32) | copy-start | bytes 3145732

commit v3 on v2

--- a/solution.py
+++ b/solution.py
@@ -62,10 +62,11 @@
     boundary, ids, qkv_weight, out_weight, inner_weight, outer_weight, gain_rows, shift_rows,
     result, summed, vectors,
     w_qkv, w_out, w_in, w_outer, info, column,
-    xb, ob, mixed, att, nlow, act, dg, one, two, inv_one, inv_two, goi, gai, gmix, probs, scale,
+    xb, ob, mixed, att, nlow, act, dg, one, two, inv, goi, gai, gmix, probs, scale,
     bias, gatt, hold, dkv, strip, mine, sib, rsb, vec, slots,
+    peer_act, peer_nlow, peer_att, peer_in, peer_goi, peer_dg, peer_gai, peer_gmix,
     weight_sem, in_sem, out_sem, x_send, x_recv, y_send, y_recv, sib_send, sib_recv, rs_send, rs_recv,
-    ag_send, ag_recv, slot_send, slot_recv, pass_send, pass_recv, own_sem,
+    ag_send, ag_recv, slot_send, slot_recv, pass_send, pass_recv, own_sem, peer_send, peer_recv,
 ):
     blocks = BLOCKS
     micro, local = boundary.shape[1], boundary.shape[3]
@@ -120,7 +121,8 @@
         )
     ]
     vec[...] = jnp.zeros_like(vec)
-    mixed[...] = jnp.zeros_like(mixed)
+    for unit in range(units):
+        mixed[(unit + 1) * rows : (unit + 1) * rows + 80] = jnp.zeros((80, 3 * width), BF16)
     barrier = pltpu.get_barrier_semaphore()
     for other in (across, beside, sibling, ahead, behind):
         pl.semaphore_signal(barrier, inc=1, device_id=other, device_id_type=MESH)
@@ -184,7 +186,7 @@
         lane = lax.broadcasted_iota(jnp.int32, scaled_qkv.shape, 1)
         mixed[span] = jnp.where(lane < width, scaled_qkv * 0.125, scaled_qkv).astype(BF16)
         for index, (first, size, begin) in enumerate(blocks):
-            turned = pltpu.roll(info[0:8], length - begin_of(unit) - begin, 1)[0:micro, 0:WINDOW]
+            turned = pltpu.roll(info[...], length - begin_of(unit) - begin, 1)[0:micro, 0:WINDOW]
             near_ids = jnp.where(unit < 2, turned[0:1], turned[1:2])
             inside = lax.broadcasted_iota(jnp.int32, near_ids.shape, 1) < rows - begin
             near_ids = jnp.where(inside, near_ids, -1.0)
@@ -226,7 +228,7 @@
 
         scaled, inverse = normalize(xb[section, span].astype(F32) + mul(att[span], w_out[...]))
         one[span] = scaled
-        inv_one[span] = inverse
+        inv[span, 0:1] = inverse
         normed = scaled * gains[0:1] + shifts[0:1]
         hold[...] = normed
         low = normed.astype(BF16)
@@ -247,7 +249,7 @@
             inner = ahead_inner
         scaled, inverse = normalize(outer)
         two[span] = scaled
-        inv_two[span] = inverse
+        inv[span, 1:2] = inverse
         ob[section, span] = (scaled * gains[1:2] + shifts[1:2]).astype(BF16)
 
     def backward_norm(unit):
@@ -256,7 +258,7 @@
         scaled = two[span]
         vec[1:2] += jnp.sum(upstream * scaled, axis=0, keepdims=True)
         vec[3:4] += jnp.sum(upstream, axis=0, keepdims=True)
-        grad_two = normalize_back(upstream, scaled, inv_two[span], gains[1:2])
+        grad_two = normalize_back(upstream, scaled, inv[span, 1:2], gains[1:2])
         hold[...] = grad_two
         goi[span] = grad_two.astype(BF16)
 
@@ -284,7 +286,7 @@
         scaled = one[span]
         vec[0:1] += jnp.sum(total * scaled, axis=0, keepdims=True)
         vec[2:3] += jnp.sum(total, axis=0, keepdims=True)
-        grad_one = normalize_back(total, scaled, inv_one[span], gains[0:1])
+        grad_one = normalize_back(total, scaled, inv[span, 0:1], gains[0:1])
         hold[...] = grad_one
         low = grad_one.astype(BF16)
         gai[span] = low
@@ -327,12 +329,96 @@
             return 0
 
         lax.fori_loop(0, width // 128, pair_step, 0, unroll=True)
+
+    def backward_input(unit):
+        span = unit_rows(unit)
         ob[1 - section, span] = (hold[...] + against(gmix[span], w_qkv[...])).astype(BF16)
 
     def backward(unit):
         backward_norm(unit)
         backward_feed(unit)
         backward_rest(unit)
+        backward_input(unit)
+
+    half = 1024
+    seg = half // chips
+
+    def spare(group, way, index):
+        tile = way * 2 + index
+        if group == 2:
+            return mixed.at[pl.ds(0, 512), pl.ds(tile * 256, 256)]
+        return probs.at[pl.ds(0, 512), pl.ds((group * 4 + tile) * 256, 256)]
+
+    def sib_copy(group, way, index):
+        return pltpu.make_async_remote_copy(
+            src_ref=spare(group, way, index), dst_ref=sib.at[group, way, pl.ds(index * 512, 512)],
+            send_sem=sib_send.at[group, way, index], recv_sem=sib_recv.at[group, way, index],
+            device_id=sibling, device_id_type=MESH,
+        )
+
+    def block_of(group, block, span):
+        cols = pl.ds(pl.multiple_of(block * 512, 512), 512)
+        if group == 0:
+            return contract(act[span, cols], goi[span])
+        if group == 1:
+            return contract(nlow[span], dg[span, cols])
+        cols = pl.ds(pl.multiple_of(jnp.maximum(block - 1, 0) * 512, 512), 512)
+        left = jnp.where(block == 0, att[span], xb[section, span])
+        return contract(left, jnp.where(block == 0, gai[span], gmix[span, cols]))
+
+    def both(own, peer):
+        return jnp.concatenate([own, peer], axis=0)
+
+    def last_block(group, index):
+        span = pl.ds((units - 1) * rows, rows)
+        block = core * 2 + index
+        cols = pl.ds(pl.multiple_of(block * 512, 512), 512)
+        here = slice(index * 512, (index + 1) * 512)
+        if group == 0:
+            return contract(both(act[span, cols], peer_act[:, here]), both(goi[span], peer_goi[...]))
+        if group == 1:
+            return contract(both(nlow[span], peer_nlow[...]), both(dg[span, cols], peer_dg[:, here]))
+        cols = pl.ds(pl.multiple_of(jnp.maximum(block - 1, 0) * 512, 512), 512)
+        first = block == 0
+        peer_cols = pl.ds(pl.multiple_of(jnp.where(first, 0, (core + index - 1) * 512), 512), 512)
+        left = jnp.where(first, both(att[span], peer_att[...]), both(xb[section, span], peer_in[...]))
+        right = jnp.where(first, both(gai[span], peer_gai[...]), both(gmix[span, cols], peer_gmix[:, peer_cols]))
+        return contract(left, right)
+
+    def peer_copy(index):
+        span = pl.ds((units - 1) * rows, rows)
+        wide = pl.ds(pl.multiple_of((1 - core) * 1024, 512), 1024)
+        near = pl.ds(pl.multiple_of((1 - core) * 512, 512), 1024)
+        source, target = (
+            (act.at[span, wide], peer_act), (nlow.at[span], peer_nlow), (att.at[span], peer_att),
+            (xb.at[section, span], peer_in), (goi.at[span], peer_goi), (dg.at[span, wide], peer_dg),
+            (gai.at[span], peer_gai), (gmix.at[span, near], peer_gmix),
+        )[index]
+        return pltpu.make_async_remote_copy(
+            src_ref=source, dst_ref=target, send_sem=peer_send.at[index], recv_sem=peer_recv.at[index],
+            device_id=sibling, device_id_type=MESH,
+        )
+
+    def put(room, part, first):
+        room[...] = (part if first else part + room[...].astype(F32)).astype(BF16)
+
+    def fill_own(group, span, first):
+        for index in range(2):
+            value = block_of(group, core * 2 + index, span)
+            for way in range(2):
+                room = mine.at[group, way, pl.ds(index * 512, 512)]
+                put(room, value[:, way * 256 : (way + 1) * 256], first)
+
+    def fill_other(group, span, first):
+        for index in range(2):
+            value = block_of(group, (1 - core) * 2 + index, span)
+            for way in range(2):
+                put(spare(group, way, index), value[:, way * 256 : (way + 1) * 256], first)
+
+    def sib_start(group):
+        for way in range(2):
+            for index in range(2):
+                sib_copy(group, way, index).start()
 
     def slot_step(slot, _):
         is_forward = jnp.where(section == 0, slot < units, lax.rem(slot, 2) == 0)
@@ -369,6 +455,23 @@
             @pl.when(section == 1)
             def _():
                 x_copy(unit).start()
+
+            @pl.when(jnp.logical_and(section == 0, unit == 0))
+            def _():
+                for group in range(GROUPS):
+                    fill_own(group, pl.ds(0, rows), True)
+
+            @pl.when(jnp.logical_and(section == 0, unit == 1))
+            def _():
+                for group in range(GROUPS):
+                    fill_other(group, pl.ds(0, 2 * rows), True)
+
+            return None
+
+        @pl.when(jnp.logical_and(is_forward, unit == units - 1))
+        def _():
+            for index in range(4):
+                peer_copy(index).start()
 
         return 0
 
@@ -390,7 +493,7 @@
             parts = ((odd + REACH, 0, shift - REACH), (even, shift - REACH, rows))
         return [
             pltpu.make_async_copy(
-                ob.at[1, pl.ds(source, size)], result.at[0, group, 0, pl.ds(target, size)],
+                ob.at[1, pl.ds(source, size)], result.at[group, pl.ds(target, size)],
                 out_sem.at[group, index],
             )
             for index, (source, target, size) in enumerate(parts)
@@ -415,61 +518,14 @@
                     for part in outputs(group, side):
                         part.start()
 
-    half = 1024
-    seg = half // chips
-
-    def spare(group, way, index):
-        tile = way * 2 + index
-        if group == 2:
-            return mixed.at[pl.ds(0, 512), pl.ds(tile * 256, 256)]
-        return probs.at[pl.ds(0, 512), pl.ds((group * 4 + tile) * 256, 256)]
-
-    def sib_copy(group, way, index):
-        return pltpu.make_async_remote_copy(
-            src_ref=spare(group, way, index), dst_ref=sib.at[group, way, pl.ds(index * 512, 512)],
-            send_sem=sib_send.at[group, way, index], recv_sem=sib_recv.at[group, way, index],
-            device_id=sibling, device_id_type=MESH,
-        )
-
-    def block_of(group, block, span):
-        cols = pl.ds(pl.multiple_of(block * 512, 512), 512)
-        if group == 0:
-            return contract(act[span, cols], goi[span])
-        if group == 1:
-            return contract(nlow[span], dg[span, cols])
-        cols = pl.ds(pl.multiple_of(jnp.maximum(block - 1, 0) * 512, 512), 512)
-        left = jnp.where(block == 0, att[span], xb[section, span])
-        return contract(left, jnp.where(block == 0, gai[span], gmix[span, cols]))
-
-    early, late = pl.ds(0, (units - 1) * rows), pl.ds((units - 1) * rows, rows)
-
-    def prepare(group):
-        for index in range(2):
-            value = block_of(group, (1 - core) * 2 + index, early).astype(BF16)
-            for way in range(2):
-                spare(group, way, index)[...] = value[:, way * 256 : (way + 1) * 256]
-        for index in range(2):
-            value = block_of(group, core * 2 + index, early).astype(BF16)
-            for way in range(2):
-                mine[group, way, index * 512 : (index + 1) * 512] = value[:, way * 256 : (way + 1) * 256]
-
-    def others(group):
-        for index in range(2):
-            value = block_of(group, (1 - core) * 2 + index, late)
-            for way in range(2):
-                part = value[:, way * 256 : (way + 1) * 256]
-                room = spare(group, way, index)
-                room[...] = (room[...].astype(F32) + part).astype(BF16)
-                sib_copy(group, way, index).start()
-
     def ours(group):
         for index in range(2):
-            value = block_of(group, core * 2 + index, late)
+            value = last_block(group, index)
+            span = slice(index * 512, (index + 1) * 512)
             for way in range(2):
                 sib_copy(group, way, index).wait_recv()
                 part = value[:, way * 256 : (way + 1) * 256]
-                span = slice(index * 512, (index + 1) * 512)
-                total = mine[group, way, span].astype(F32) + part + sib[group, way, span].astype(F32)
+                total = part + mine[group, way, span].astype(F32) + sib[group, way, span].astype(F32)
                 mine[group, way, span] = total.astype(BF16)
 
     def segment(position):
@@ -564,37 +620,60 @@
         lax.fori_loop(0, 2, each, 0)
 
     last = units - 1
-    for group in range(GROUPS):
-        prepare(group)
+    @pl.when(section == 0)
+    def _():
+        for group in range(GROUPS):
+            fill_other(group, pl.ds(2 * rows, rows), False)
+            sib_start(group)
+        for group in range(GROUPS):
+            fill_own(group, pl.ds(rows, 2 * rows), False)
+
+    @pl.when(section == 1)
+    def _():
+        for group in range(GROUPS):
+            fill_other(group, pl.ds(0, 3 * rows), True)
+            sib_start(group)
+        for group in range(GROUPS):
+            fill_own(group, pl.ds(0, 3 * rows), True)
 
     @pl.when(section == 0)
     def _():
         x_copy(last).wait_recv()
         backward_norm(last)
 
-    others(0)
+    peer_copy(4).start()
 
     @pl.when(section == 0)
     def _():
         backward_feed(last)
 
-    others(1)
-    ours(0)
-    serve(0, 0)
+    peer_copy(5).start()
 
     @pl.when(section == 0)
     def _():
         backward_rest(last)
 
+    peer_copy(6).start()
+    peer_copy(7).start()
+    vec_copy.start()
+    for index in range(5):
+        peer_copy(index).wait_recv()
+    ours(0)
+    serve(0, 0)
+    peer_copy(5).wait_recv()
+    ours(1)
+    serve(1, 0)
+    peer_copy(6).wait_recv()
+    peer_copy(7).wait_recv()
+    ours(2)
+    serve(2, 0)
+
+    @pl.when(section == 0)
+    def _():
+        backward_input(last)
+
     for group in range(micro):
         strip_copy(group).start()
-    vec_copy.start()
-    others(2)
-    ours(1)
-    serve(1, 0)
-    ours(2)
-    serve(2, 0)
-    finish()
     vec_copy.wait()
     slots[0] = vec[0:8] + vec[8:16]
 
@@ -616,12 +695,16 @@
 
         return 0
 
-    lax.fori_loop(1, 2 * chips - 1, round_step, 0)
+    lax.fori_loop(1, 4, round_step, 0)
+    finish()
+    lax.fori_loop(4, 2 * chips - 1, round_step, 0)
     slot_copy(chips - 2).wait_recv()
     total = jnp.zeros((8, width), F32)
     for position in range(chips):
         total = total + slots[around(place - position)]
-    vectors[...] = total
+    vec[0:8] = total
+    told = pltpu.make_async_copy(vec.at[pl.ds(0, 8)], vectors.at[pl.ds(0, 8)], in_sem.at[0])
+    told.start()
 
     def drain(flat, _):
         group, way = lax.div(flat, 2), lax.rem(flat, 2)
@@ -647,6 +730,8 @@
         for way in range(2):
             for index in range(2):
                 sib_copy(group, way, index).wait_send()
+    for index in range(8):
+        peer_copy(index).wait_send()
 
     def drain_slots(step, _):
         slot_copy(step).wait_send()
@@ -659,6 +744,7 @@
         return 0
 
     lax.fori_loop(0, units, drain_units, 0)
+    told.wait()
     for group in range(micro):
         halo(group).wait_send()
         strip_copy(group).wait_send()
@@ -670,30 +756,51 @@
                     part.wait()
 
 
-def widen(summed, vectors, qkv, out, inner, outer, gain, shift, narrow, wide, in_sem, out_sem):
-    homes = [outer.at[0, pl.ds(index * 512, 512)] for index in range(4)]
-    homes += [inner.at[0, :, pl.ds(index * 512, 512)] for index in range(4)]
-    homes += [out.at[0]] + [qkv.at[0, :, pl.ds(index * 512, 512)] for index in range(3)]
+def widen(summed, vectors, merged, qkv, out, inner, outer, gain, shift, result, narrow, wide, held, rows, in_sem, out_sem, rest_sem):
+    homes = []
+    for index in range(8):
+        homes.append(outer.at[0, pl.ds(index * 256, 256)])
+    for column in range(4):
+        for part in range(2):
+            homes.append(inner.at[0, pl.ds(part * 256, 256), pl.ds(column * 512, 512)])
+    for part in range(2):
+        homes.append(out.at[0, pl.ds(part * 256, 256)])
+    for column in range(3):
+        for part in range(2):
+            homes.append(qkv.at[0, pl.ds(part * 256, 256), pl.ds(column * 512, 512)])
     loads = [
         pltpu.make_async_copy(
-            summed.at[index // 4, :, pl.ds(index % 4 * 512, 512)], narrow.at[index], in_sem.at[index]
+            summed.at[index // 8, :, pl.ds(index % 8 * 256, 256)], narrow.at[index], in_sem.at[index]
         )
         for index in range(len(homes))
     ]
     stores = [
         pltpu.make_async_copy(wide.at[index], home, out_sem.at[index]) for index, home in enumerate(homes)
     ]
+    firsts = [
+        pltpu.make_async_copy(merged.at[pl.ds(0, held.shape[0])], held, rest_sem.at[0]),
+        pltpu.make_async_copy(vectors.at[pl.ds(0, 8)], rows, rest_sem.at[1]),
+    ]
+    seconds = [
+        pltpu.make_async_copy(held, result.at[0, :, 0], rest_sem.at[2]),
+        pltpu.make_async_copy(rows.at[pl.ds(0, 2)], gain.at[0], rest_sem.at[3]),
+        pltpu.make_async_copy(rows.at[pl.ds(2, 2)], shift.at[0], rest_sem.at[4]),
+    ]
     for load in loads:
         load.start()
-    gain[0] = vectors[0:2]
-    shift[0] = vectors[2:4]
+    for copy_of in firsts:
+        copy_of.start()
     for index, (load, store) in enumerate(zip(loads, stores)):
         load.wait()
         for way in range(2):
             wide[index, :, way * 256 : (way + 1) * 256] = narrow[index, way].astype(F32)
         store.start()
-    for store in stores:
-        store.wait()
+    for copy_of in firsts:
+        copy_of.wait()
+    for copy_of in seconds:
+        copy_of.start()
+    for copy_of in stores + seconds:
+        copy_of.wait()
 
 
 def per_device(mesh, boundary, sentence_ids, qkv_weight, out_weight, inner_weight, outer_weight, norm_gain, norm_bias):
@@ -711,19 +818,19 @@
     result, summed, vectors = pl.pallas_call(
         functools.partial(kernel, units, rows, chips, width, inner_width),
         out_shape=(
-            jax.ShapeDtypeStruct(boundary.shape, BF16),
+            jax.ShapeDtypeStruct((4 * micro, local, width), BF16),
             jax.ShapeDtypeStruct((GROUPS, 2, 2048, 256), BF16),
-            jax.ShapeDtypeStruct((8, width), F32),
+            jax.ShapeDtypeStruct((2048, width), F32),
         ),
         in_specs=[any_space, vmem] + [any_space] * 4 + [vmem] * 2,
-        out_specs=(any_space, any_space, vmem),
+        out_specs=(any_space, any_space, any_space),
         scratch_shapes=[
             pltpu.VMEM((width, 3 * width), BF16),
             pltpu.VMEM((width, width), BF16),
             pltpu.VMEM((width, inner_width), BF16),
             pltpu.VMEM((inner_width, width), BF16),
-            pltpu.VMEM((128, length), F32),
-            pltpu.VMEM((length, 128), F32),
+            pltpu.VMEM((8, length), F32),
+            pltpu.VMEM((length, 8), F32),
             pltpu.VMEM((2, tokens, width), BF16),
             pltpu.VMEM((2, tokens, width), BF16),
             pltpu.VMEM((tokens + 80, 3 * width), BF16),
@@ -733,8 +840,7 @@
             pltpu.VMEM((tokens, inner_width), BF16),
             pltpu.VMEM((tokens, width), F32),
             pltpu.VMEM((tokens, width), F32),
-            pltpu.VMEM((tokens, 1), F32),
-            pltpu.VMEM((tokens, 1), F32),
+            pltpu.VMEM((tokens, 2), F32),
             pltpu.VMEM((tokens, width), BF16),
             pltpu.VMEM((tokens, width), BF16),
             pltpu.VMEM((tokens, 3 * width), BF16),
@@ -750,31 +856,42 @@
             pltpu.VMEM((GROUPS, 2, hops, 1024 // chips, 256), BF16),
             pltpu.VMEM((16, width), F32),
             pltpu.VMEM((chips, 8, width), F32),
+            pltpu.VMEM((rows, 1024), BF16),
+            pltpu.VMEM((rows, width), BF16),
+            pltpu.VMEM((rows, width), BF16),
+            pltpu.VMEM((rows, width), BF16),
+            pltpu.VMEM((rows, width), BF16),
+            pltpu.VMEM((rows, 1024), BF16),
+            pltpu.VMEM((rows, width), BF16),
+            pltpu.VMEM((rows, 1024), BF16),
             dma((4,)), dma((units,)), dma((micro, 2)), dma((units,)), dma((units,)),
             dma((2 * micro,)), dma((2 * micro,)), dma((GROUPS, 2, 2)), dma((GROUPS, 2, 2)),
             dma((GROUPS, 2, hops)), dma((GROUPS, 2, hops)), dma((GROUPS, 2, hops)), dma((GROUPS, 2, hops)),
             dma((chips + 1,)), dma((chips + 1,)), dma((GROUPS, 2)), dma((GROUPS, 2)), dma((GROUPS, 2)),
+            dma((8,)), dma((8,)),
         ],
         compiler_params=pltpu.CompilerParams(
             collective_id=0, has_side_effects=True, vmem_limit_bytes=63 * 1024 * 1024
         ),
     )(boundary, sentence_ids, qkv_weight, out_weight, inner_weight, outer_weight, norm_gain, norm_bias)
 
-    blocks = 4 * GROUPS
-    grad_qkv, grad_out, grad_inner, grad_outer, grad_gain, grad_bias = pl.pallas_call(
+    blocks = 8 * GROUPS
+    hbm = pl.BlockSpec(memory_space=pltpu.HBM)
+    grad_qkv, grad_out, grad_inner, grad_outer, grad_gain, grad_bias, result = pl.pallas_call(
         widen,
         out_shape=tuple(
             jax.ShapeDtypeStruct(item.shape, F32)
             for item in (qkv_weight, out_weight, inner_weight, outer_weight, norm_gain, norm_bias)
-        ),
-        in_specs=[any_space, vmem],
-        out_specs=(any_space,) * 4 + (vmem,) * 2,
+        )
+        + (jax.ShapeDtypeStruct(boundary.shape, BF16),),
+        in_specs=[hbm] * 3,
+        out_specs=(hbm,) * 7,
         scratch_shapes=[
-            pltpu.VMEM((blocks, 2, 512, 256), BF16), pltpu.VMEM((blocks, 512, 512), F32),
-            dma((blocks,)), dma((blocks,)),
+            pltpu.VMEM((blocks, 2, 256, 256), BF16), pltpu.VMEM((blocks, 256, 512), F32),
+            pltpu.VMEM((micro, local, width), BF16), pltpu.VMEM((8, width), F32), dma((blocks,)), dma((blocks,)), dma((5,)),
         ],
-        compiler_params=pltpu.CompilerParams(vmem_limit_bytes=48 * 1024 * 1024),
-    )(summed, vectors)
+        compiler_params=pltpu.CompilerParams(vmem_limit_bytes=62 * 1024 * 1024),
+    )(summed, vectors, result)
     return (result, grad_qkv, grad_out, grad_inner, grad_outer, grad_gain, grad_bias)
 
 

time: 153 us -> 148 us (0.967)
  Pallas kernels: 151 us -> 147 us
  local copies, waits for them, and re-layouts: 1.69 us -> 0 us
    pallas_call x1, Pallas kernels: 144 us -> 139 us  [per_device(): pl.pallas_call(functools.partial(kernel, units, rows, chips, width, inner...]
    unnamed x5 -> x0, local copies, waits for them, and re-layouts: 1.69 us -> none
where the time goes in v3:
time: 148 us; the launch traced here: 147 us
  Pallas kernels  147 us (99%)
    pallas_call x1, Pallas kernels, per_device(): pl.pallas_call(functools.partial(kernel, units, rows, chips, width, inner...  139 us
    pallas_call x1, Pallas kernels, per_device(): pl.pallas_call(widen, out_shape=tuple((jax.ShapeDtypeStruct(item.shape, F...  7.51 us

profile of v3, /device:TPU:0, one launch (start us, length us, event | category | flops | bytes accessed | tf_op | source)
XLA Modules:
  0.0 147.4 jit_solution(16475360984625844812)
XLA Ops:
  0.6 139.1 %shard_map.135 = (bf16[8,512,512]{2,1,0:T(8,128)(2,1)}, bf16[3,2,2048,256]{3,2,1,0:T(8,128)(2,1)}, f32[2048,512]{1,0:T(8,128)}) custom-call(bf16[1,2,1,512,512]{4,3,2,1,0:T(8,128)(2,1)} %boundary.1, s32[2,1,1024]{2,1,0:T(1,128)} %ids.1, bf16[1,512,1536]{2,1,0:T(8,128)(2,1)} %qkv_weight.1, bf16[1,512,512]{2,1,0:T(8,128)(2,1)} %out_weight.1, ...), custom_call_target="tpu_custom_call" | custom-call | tf_op jit(solution)/shard_map/pallas_call | solution.py:818
  139.7 7.5 %shard_map.136 = (f32[1,512,1536]{2,1,0:T(8,128)}, f32[1,512,512]{2,1,0:T(8,128)}, f32[1,512,2048]{2,1,0:T(8,128)}, f32[1,2048,512]{2,1,0:T(8,128)}, f32[1,2,512...) custom-call(bf16[3,2,2048,256]{3,2,1,0:T(8,128)(2,1)} %get-tuple-element.17.summed, ...), custom_call_target="tpu_custom_call" | custom-call | tf_op jit(solution)/shard_map/pallas_call | solution.py:880

commit v4 on v3

--- a/solution.py
+++ b/solution.py
@@ -33,8 +33,8 @@
 
 def gelu(x):
     phi = 0.5 + 0.5 * lax.erf(x * 0.7071067811865476)
-    bell = jnp.exp(x * x * -0.5) * 0.3989422804014327
-    return (x * phi).astype(BF16), (phi + x * bell).astype(BF16)
+    bell = jnp.exp2(x * x * -0.7213475204444817)
+    return (x * phi).astype(BF16), (phi + x * 0.3989422804014327 * bell).astype(BF16)
 
 
 def normalize(resid):
@@ -63,7 +63,7 @@
     result, summed, vectors,
     w_qkv, w_out, w_in, w_outer, info, column,
     xb, ob, mixed, att, nlow, act, dg, one, two, inv, goi, gai, gmix, probs, scale,
-    bias, gatt, hold, dkv, strip, mine, sib, rsb, vec, slots,
+    bias, gatt, hold, strip, mine, sib, rsb, vec, slots,
     peer_act, peer_nlow, peer_att, peer_in, peer_goi, peer_dg, peer_gai, peer_gmix,
     weight_sem, in_sem, out_sem, x_send, x_recv, y_send, y_recv, sib_send, sib_recv, rs_send, rs_recv,
     ag_send, ag_recv, slot_send, slot_recv, pass_send, pass_recv, own_sem, peer_send, peer_recv,
@@ -120,18 +120,17 @@
             ((qkv_weight, w_qkv), (out_weight, w_out), (inner_weight, w_in), (outer_weight, w_outer))
         )
     ]
+    load(0).start()
+    for weight in weights:
+        weight.start()
+    for unit in range(1, units):
+        load(unit).start()
     vec[...] = jnp.zeros_like(vec)
     for unit in range(units):
         mixed[(unit + 1) * rows : (unit + 1) * rows + 80] = jnp.zeros((80, 3 * width), BF16)
     barrier = pltpu.get_barrier_semaphore()
     for other in (across, beside, sibling, ahead, behind):
         pl.semaphore_signal(barrier, inc=1, device_id=other, device_id_type=MESH)
-    load(0).start()
-    weights[0].start()
-    for unit in range(1, units):
-        load(unit).start()
-    for weight in weights[1:]:
-        weight.start()
 
     spot = lax.broadcasted_iota(jnp.int32, (micro, length), 1)
     sentence = ids[:, 0, :]
@@ -182,9 +181,8 @@
         span = unit_rows(unit)
         start = pl.multiple_of(unit * rows, 16)
         hidden = xb[section, span]
-        scaled_qkv = mul(hidden, w_qkv[...])
-        lane = lax.broadcasted_iota(jnp.int32, scaled_qkv.shape, 1)
-        mixed[span] = jnp.where(lane < width, scaled_qkv * 0.125, scaled_qkv).astype(BF16)
+        mixed[span, 0:width] = (mul(hidden, w_qkv[:, 0:width]) * 0.125).astype(BF16)
+        mixed[span, width:] = mul(hidden, w_qkv[:, width:]).astype(BF16)
         for index, (first, size, begin) in enumerate(blocks):
             turned = pltpu.roll(info[...], length - begin_of(unit) - begin, 1)[0:micro, 0:WINDOW]
             near_ids = jnp.where(unit < 2, turned[0:1], turned[1:2])
@@ -233,7 +231,7 @@
         hold[...] = normed
         low = normed.astype(BF16)
         nlow[span] = low
-        tile = 512
+        tile = 256
         count = inner_width // tile
         inner = mul(nlow[span], w_in[:, 0:tile])
         outer = hold[...]
@@ -259,15 +257,15 @@
         vec[1:2] += jnp.sum(upstream * scaled, axis=0, keepdims=True)
         vec[3:4] += jnp.sum(upstream, axis=0, keepdims=True)
         grad_two = normalize_back(upstream, scaled, inv[span, 1:2], gains[1:2])
-        hold[...] = grad_two
         goi[span] = grad_two.astype(BF16)
-
-    def backward_feed(unit):
+        return grad_two
+
+    def backward_feed(unit, grad_two):
         span = unit_rows(unit)
         tile = 512
         count = inner_width // tile
         grad_active = against(goi[span], w_outer[0:tile])
-        total = hold[...]
+        total = grad_two
         for step in range(count):
             next_active = None
             if step + 1 < count:
@@ -277,12 +275,11 @@
             dg[span, cols] = grad_inner
             total = total + against(grad_inner, w_in[:, step * tile : (step + 1) * tile])
             grad_active = next_active
-        hold[...] = total
-
-    def backward_rest(unit):
+        return total
+
+    def backward_rest(unit, total):
         span = unit_rows(unit)
         start = pl.multiple_of(unit * rows, 16)
-        total = hold[...]
         scaled = one[span]
         vec[0:1] += jnp.sum(total * scaled, axis=0, keepdims=True)
         vec[2:3] += jnp.sum(total, axis=0, keepdims=True)
@@ -296,7 +293,7 @@
             lanes = pl.multiple_of(pair * 128, 128)
             key_lanes = pl.ds(pl.multiple_of(width + pair * 128, 128), 128)
             value_lanes = pl.ds(pl.multiple_of(2 * width + pair * 128, 128), 128)
-            dkv[...] = jnp.zeros_like(dkv)
+            parts = ([], [])
             for first, size, begin in blocks:
                 near = pl.ds(pl.multiple_of(start + begin, 16), WINDOW)
                 own = pl.ds(pl.multiple_of(start + first, 16), size)
@@ -319,13 +316,16 @@
                 gmix[own, pl.ds(lanes, 128)] = (grad_query * 0.125).astype(BF16)
                 for kind, (small, sides) in enumerate(((mixed[own, pl.ds(lanes, 128)], grads), (grad_pair, share))):
                     turned = small.T
-                    for head in range(2):
-                        heads = slice(head * 64, (head + 1) * 64)
-                        dkv[kind, heads, begin : begin + WINDOW] += mul(
-                            turned[heads], sides[head * size : (head + 1) * size]
-                        )
-            gmix[span, key_lanes] = dkv[0].astype(BF16).T[0:rows]
-            gmix[span, value_lanes] = dkv[1].astype(BF16).T[0:rows]
+                    heads = [
+                        mul(turned[head * 64 : (head + 1) * 64], sides[head * size : (head + 1) * size])
+                        for head in range(2)
+                    ]
+                    parts[kind].append(jnp.concatenate(heads, axis=0))
+            for kind, home in enumerate((key_lanes, value_lanes)):
+                low, high = parts[kind]
+                middle = low[:, 128:] + high[:, :128]
+                whole = jnp.concatenate([low[:, :128], middle, high[:, 128:]], axis=1)
+                gmix[span, home] = whole.astype(BF16).T[0:rows]
             return 0
 
         lax.fori_loop(0, width // 128, pair_step, 0, unroll=True)
@@ -335,9 +335,7 @@
         ob[1 - section, span] = (hold[...] + against(gmix[span], w_qkv[...])).astype(BF16)
 
     def backward(unit):
-        backward_norm(unit)
-        backward_feed(unit)
-        backward_rest(unit)
+        backward_rest(unit, backward_feed(unit, backward_norm(unit)))
         backward_input(unit)
 
     half = 1024
@@ -639,19 +637,19 @@
     @pl.when(section == 0)
     def _():
         x_copy(last).wait_recv()
-        backward_norm(last)
+        hold[...] = backward_norm(last)
 
     peer_copy(4).start()
 
     @pl.when(section == 0)
     def _():
-        backward_feed(last)
+        hold[...] = backward_feed(last, hold[...])
 
     peer_copy(5).start()
 
     @pl.when(section == 0)
     def _():
-        backward_rest(last)
+        backward_rest(last, hold[...])
 
     peer_copy(6).start()
     peer_copy(7).start()
@@ -849,7 +847,6 @@
             pltpu.VMEM((rows, WINDOW), F32),
             pltpu.VMEM((rows, width), BF16),
             pltpu.VMEM((rows, width), F32),
-            pltpu.VMEM((2, 128, 384), F32),
             pltpu.VMEM((micro, REACH, width), BF16),
             pltpu.VMEM((GROUPS, 2, 1024, 256), BF16),
             pltpu.VMEM((GROUPS, 2, 1024, 256), BF16),

time: 148 us -> 147 us (level)
  no operation moved by 1% of the time
where the time goes in v4:
time: 147 us; the launch traced here: 146 us
  Pallas kernels  146 us (99%)
    pallas_call x1, Pallas kernels, per_device(): pl.pallas_call(functools.partial(kernel, units, rows, chips, width, inner...  138 us
    pallas_call x1, Pallas kernels, per_device(): pl.pallas_call(widen, out_shape=tuple((jax.ShapeDtypeStruct(item.shape, F...  7.51 us

profile of v4, /device:TPU:0, one launch (start us, length us, event | category | flops | bytes accessed | tf_op | source)
XLA Modules:
  0.0 146.5 jit_solution(13000365500448195196)
XLA Ops:
  0.6 138.1 %shard_map.135 = (bf16[8,512,512]{2,1,0:T(8,128)(2,1)}, bf16[3,2,2048,256]{3,2,1,0:T(8,128)(2,1)}, f32[2048,512]{1,0:T(8,128)}) custom-call(bf16[1,2,1,512,512]{4,3,2,1,0:T(8,128)(2,1)} %boundary.1, s32[2,1,1024]{2,1,0:T(1,128)} %ids.1, bf16[1,512,1536]{2,1,0:T(8,128)(2,1)} %qkv_weight.1, bf16[1,512,512]{2,1,0:T(8,128)(2,1)} %out_weight.1, ...), custom_call_target="tpu_custom_call" | custom-call | tf_op jit(solution)/shard_map/pallas_call | solution.py:816
  138.8 7.5 %shard_map.136 = (f32[1,512,1536]{2,1,0:T(8,128)}, f32[1,512,512]{2,1,0:T(8,128)}, f32[1,512,2048]{2,1,0:T(8,128)}, f32[1,2048,512]{2,1,0:T(8,128)}, f32[1,2,512...) custom-call(bf16[3,2,2048,256]{3,2,1,0:T(8,128)(2,1)} %get-tuple-element.17.summed, ...), custom_call_target="tpu_custom_call" | custom-call | tf_op jit(solution)/shard_map/pallas_call | solution.py:877

commit v5 on v4

--- a/solution.py
+++ b/solution.py
@@ -301,15 +301,17 @@
                 key = mixed[near, key_lanes]
                 value = mixed[near, value_lanes]
                 grad_pair = gatt[first : first + size, pl.ds(lanes, 128)]
-                paired = (grad_pair.astype(F32) * att[own, pl.ds(lanes, 128)].astype(F32)).astype(BF16)
                 grad = jnp.concatenate(halves(grad_pair), axis=0)
-                left = jnp.concatenate([grad, jnp.concatenate(halves(paired), axis=0)], axis=1)
+                inverse = scale[own, pl.ds(lanes, 128)]
+                inverse = jnp.concatenate([inverse[:, 0:1], inverse[:, 64:65]], axis=0)
                 share = jnp.concatenate(
                     [probs[own, pl.ds(pl.multiple_of(pair * 512 + head * 256, 256), 256)] for head in range(2)],
                     axis=0,
                 )
-                tilt = against(left, jnp.concatenate([value, jnp.full((WINDOW, 128), -1.0, BF16)], axis=1))
-                grads = (share.astype(F32) * tilt).astype(BF16)
+                tilt = against(grad, value)
+                held_share = share.astype(F32)
+                rowwise = jnp.sum(held_share * tilt, axis=-1, keepdims=True) * inverse
+                grads = (held_share * (tilt - rowwise)).astype(BF16)
                 wide = mul(grads, key)
                 lane = lax.broadcasted_iota(jnp.int32, (size, 128), 1)
                 grad_query = jnp.where(lane < 64, wide[:size], wide[size:])

time: 147 us -> 158 us (1.075)
  Pallas kernels: 146 us -> 157 us
    pallas_call x1, Pallas kernels: 138 us -> 149 us  [per_device(): pl.pallas_call(functools.partial(kernel, units, rows, chips, width, inner...]
where the time goes in v5:
time: 158 us; the launch traced here: 157 us
  Pallas kernels  157 us (99%)
    pallas_call x1, Pallas kernels, per_device(): pl.pallas_call(functools.partial(kernel, units, rows, chips, width, inner...  149 us
    pallas_call x1, Pallas kernels, per_device(): pl.pallas_call(widen, out_shape=tuple((jax.ShapeDtypeStruct(item.shape, F...  7.51 us

profile of v5, /device:TPU:0, one launch (start us, length us, event | category | flops | bytes accessed | tf_op | source)
XLA Modules:
  0.0 157.4 jit_solution(10207811826346583018)
XLA Ops:
  0.6 149.0 %shard_map.135 = (bf16[8,512,512]{2,1,0:T(8,128)(2,1)}, bf16[3,2,2048,256]{3,2,1,0:T(8,128)(2,1)}, f32[2048,512]{1,0:T(8,128)}) custom-call(bf16[1,2,1,512,512]{4,3,2,1,0:T(8,128)(2,1)} %boundary.1, s32[2,1,1024]{2,1,0:T(1,128)} %ids.1, bf16[1,512,1536]{2,1,0:T(8,128)(2,1)} %qkv_weight.1, bf16[1,512,512]{2,1,0:T(8,128)(2,1)} %out_weight.1, ...), custom_call_target="tpu_custom_call" | custom-call | tf_op jit(solution)/shard_map/pallas_call | solution.py:818
  149.7 7.5 %shard_map.136 = (f32[1,512,1536]{2,1,0:T(8,128)}, f32[1,512,512]{2,1,0:T(8,128)}, f32[1,512,2048]{2,1,0:T(8,128)}, f32[1,2048,512]{2,1,0:T(8,128)}, f32[1,2,512...) custom-call(bf16[3,2,2048,256]{3,2,1,0:T(8,128)(2,1)} %get-tuple-element.17.summed, ...), custom_call_target="tpu_custom_call" | custom-call | tf_op jit(solution)/shard_map/pallas_call | solution.py:879
